TPU v7x, 32 devices: a whole 2x2x4 slice. The times are simulated.
32 devices in a mesh: px: 4 (over z), pz: 8 (over y, x, core).
Axes of the slice: x: 2, y: 2, z: 4, core: 2. Of those that a mesh axis runs over, the one named last changes fastest.
Arguments:
- charge: float32 [8192, 128], P(('px', 'pz')), may hold values from -6 to 6
- dest: int32 [8192, 1], P(('px', 'pz')), may hold values from 0 to 31; in each aligned block of 256 rows (0 to 255, 256 to 511, ...) at most 16 rows name the same one
- local_ids: int32 [8192], P(('px', 'pz')), may hold values from 0 to 255
- green_hat: float32 [64, 64, 2048], P(None, 'px', 'pz'), may hold values from 0.1 to 10, as said below
Outputs:
- potential: float32 [8192, 128], P(('px', 'pz'))
Inputs may be any that keep to these rules, and one draw needn't show every extreme that they name: `dest`: among the 256 slots of one box, no pencil is named by more than 16; some pencil is named by exactly 16. green_hat is even in every dimension: its value at frequencies (k1, k2, k3) equals that at ((64 - k1) mod 2 * 32, (64 - k2) mod 2 * 32, (2048 - k3) mod 2 * 1024) taken in any single dimension.
All inputs are finite; a program needn't handle non-finite values.
Results may differ from a plain program's by a relative error of at most 0.00007.
Values sent between devices are 32-bit elements; how exact they have to be, the bound alone decides.
A program may use at most 64 MiB of HBM per device.

v0:
```python
import math

import jax
import jax.numpy as jnp
from jax import lax
from jax.sharding import PartitionSpec as P

CXP = 8
CYP = 4
NZP = 1024


def dft_table(n_in, n_out, period, sign):
    rows = lax.broadcasted_iota(jnp.int32, (n_in, n_out), 0)
    cols = lax.broadcasted_iota(jnp.int32, (n_in, n_out), 1)
    phase = (rows * cols % period).astype(jnp.float32) * (2.0 * math.pi / period)
    return (jnp.cos(phase), sign * jnp.sin(phase))


def rotate(real_part, imag_part, cosine, sine, form):
    first = jnp.einsum(form, real_part, cosine, precision=lax.Precision.HIGHEST)
    second = jnp.einsum(form, imag_part, sine, precision=lax.Precision.HIGHEST)
    third = jnp.einsum(form, imag_part, cosine, precision=lax.Precision.HIGHEST)
    fourth = jnp.einsum(form, real_part, sine, precision=lax.Precision.HIGHEST)
    return (first - second, third + fourth)


def solve_field(field, green_hat, wide_x, wide_y):
    cosine, sine = dft_table(NZP, 2 * NZP, 2 * NZP, -1.0)
    real_part = jnp.einsum("xyz,zk->xyk", field, cosine, precision=lax.Precision.HIGHEST)
    imag_part = jnp.einsum("xyz,zk->xyk", field, sine, precision=lax.Precision.HIGHEST)
    turned = lax.all_to_all(
        jnp.stack((real_part, imag_part)), "pz", split_axis=3, concat_axis=2, tiled=True
    )
    cosine, sine = dft_table(wide_y, 2 * wide_y, 2 * wide_y, -1.0)
    real_part, imag_part = rotate(turned[0], turned[1], cosine, sine, "xyk,yq->xqk")
    turned = lax.all_to_all(
        jnp.stack((real_part, imag_part)), "px", split_axis=2, concat_axis=1, tiled=True
    )
    cosine, sine = dft_table(wide_x, 2 * wide_x, 2 * wide_x, -1.0)
    real_part, imag_part = rotate(turned[0], turned[1], cosine, sine, "xyk,xq->qyk")
    real_part = real_part * green_hat
    imag_part = imag_part * green_hat
    cosine, sine = dft_table(2 * wide_x, wide_x, 2 * wide_x, 1.0)
    real_part, imag_part = rotate(real_part, imag_part, cosine, sine, "qyk,qx->xyk")
    turned = lax.all_to_all(
        jnp.stack((real_part, imag_part)), "px", split_axis=1, concat_axis=2, tiled=True
    )
    cosine, sine = dft_table(2 * wide_y, wide_y, 2 * wide_y, 1.0)
    real_part, imag_part = rotate(turned[0], turned[1], cosine, sine, "xqk,qy->xyk")
    turned = lax.all_to_all(
        jnp.stack((real_part, imag_part)), "pz", split_axis=2, concat_axis=3, tiled=True
    )
    cosine, sine = dft_table(2 * NZP, NZP, 2 * NZP, 1.0)
    result = jnp.einsum("xyk,kz->xyz", turned[0], cosine, precision=lax.Precision.HIGHEST)
    result = result - jnp.einsum("xyk,kz->xyz", turned[1], sine, precision=lax.Precision.HIGHEST)
    return result * (1.0 / (8.0 * wide_x * wide_y * NZP))


def local(charge, dest, local_ids, green_hat):
    n_dev = lax.axis_size(("px", "pz"))
    wide_x = CXP * lax.axis_size("px")
    wide_y = CYP * lax.axis_size("pz")
    pencil_blocks = CXP * CYP * NZP // 128
    route = dest[:, 0]
    dense = (
        jnp.zeros((n_dev * pencil_blocks, 128), jnp.float32)
        .at[route * pencil_blocks + local_ids]
        .add(charge)
    )
    pencil = lax.psum_scatter(dense, ("px", "pz"), scatter_dimension=0, tiled=True)
    field = pencil.reshape(CXP, CYP, NZP)
    phi = solve_field(field, green_hat, wide_x, wide_y)
    phi_blocks = phi.reshape(pencil_blocks, 128)
    whole = lax.all_gather(phi_blocks, ("px", "pz"), axis=0, tiled=True)
    return whole[route * pencil_blocks + local_ids]


def solution(mesh):
    return jax.shard_map(
        local,
        mesh=mesh,
        in_specs=(
            P(("px", "pz"), None),
            P(("px", "pz"), None),
            P(("px", "pz")),
            P(None, "px", "pz"),
        ),
        out_specs=P(("px", "pz"), None),
        check_vma=False,
    )
```

profile of v0, /device:TPU:0, one launch (start us, length us, event | category | flops | bytes accessed | tf_op | source)
XLA Modules:
  0.0 505.6 jit_solution(6894336540151404284)
XLA Ops:
  6.5 0.7 broadcast_multiply_fusion
  7.2 0.7 compare_select_fusion
  7.9 3.9 scatter_custom_fusion
  11.9 143.5 %reduce-scatter.2.cloned.1.call-done = f32[256,128]{1,0:T(8,128)} async-done(((f32[8192,128]{1,0:T(8,128)}), f32[256,128]{1,0:T(8,128)}) %reduce-scatter.2.cloned.1.call-update) | async-done | bytes 131088 | tf_op jit(solution)/shard_map/reduce_scatter | solution.py:71
  155.4 0.9 reshape.24
  156.4 35.7 %fusion.30 = f32[1,8,4,2048]{3,1,2,0:T(8,128)S(1)} fusion(f32[8,4,1024]{2,1,0:T(4,128)S(1)} %reshape.24), kind=kOutput, calls=%fused_computation.34 | convolution fusion | flops 834666496 | bytes 393216 | tf_op jit(solution)/shard_map/xyz,zk->xyk/dot_general | solution.py:30
  192.1 36.1 %fusion.33 = f32[1,8,4,2048]{3,1,2,0:T(8,128)S(1)} fusion(f32[8,4,1024]{2,1,0:T(4,128)S(1)} %reshape.24), kind=kOutput, calls=%fused_computation.35 | convolution fusion | flops 836763648 | bytes 393216 | tf_op jit(solution)/shard_map/xyz,zk->xyk/dot_general | solution.py:31
  228.2 5.8 %copy.30 = f32[2,8,4,2048]{1,2,0,3:T(4,128)} copy(f32[2,8,4,2048]{3,1,2,0:T(8,128)S(1)} %pad_maximum_fusion.2) | data formatting | bytes 1048576 | tf_op jit(solution)/shard_map/stack | solution.py:33
  234.0 11.4 %reshape.54 = f32[8,1,16384]{2,1,0:T(1,128)S(1)} reshape(f32[2048,2,4,8]{3,2,1,0:T(4,128)} %bitcast.123) | data formatting | bytes 1048576
  245.5 12.6 %all_to_all.60 = f32[8,1,16384]{2,1,0:T(1,128)S(1)} all-to-all(f32[8,1,16384]{2,1,0:T(1,128)S(1)} %reshape.54), channel_id=1, replica_groups=mesh['px'=4,'pz'=8] {'pz'}, dimensions={0} | all-to-all | bytes 1048576 | tf_op jit(solution)/shard_map/all_to_all | solution.py:32
  258.1 0.5 broadcast.213
  258.6 1.9 reduce
  260.5 13.1 %reshape.55 = f32[2048,2,4,8]{3,2,1,0:T(4,128)} reshape(f32[8,16384]{1,0:T(8,128)S(1)} %reduce) | data formatting | bytes 1048576
  273.6 6.7 %copy.31 = f32[2,8,4,8,256]{4,2,3,1,0:T(4,128)S(1)} copy(f32[2,8,4,8,256]{1,2,0,4,3:T(4,128)} %bitcast.124) | data formatting | bytes 1048576 | tf_op jit(solution)/shard_map/all_to_all | solution.py:32
  280.3 0.1 squeeze.25
  280.4 0.7 fusion.74
  281.1 0.1 squeeze.26
  281.2 0.7 fusion.72
  282.0 0.7 fusion.43
  282.7 0.7 fusion.42
  283.4 0.1 pad_maximum_fusion
  283.5 0.6 copy.32
  284.1 27.9 %all_to_all.61 = f32[2,8,64,256]{3,1,0,2:T(8,128)S(1)} all-to-all(f32[2,8,64,256]{3,1,0,2:T(8,128)S(1)} %copy.32), channel_id=1, replica_groups=mesh['px'=4,'pz'=8] {'px'}, dimensions={2} | all-to-all | bytes 2097152 | tf_op jit(solution)/shard_map/all_to_all | solution.py:37
  312.0 0.1 copy.51
  312.1 1.1 fusion.52
  313.3 1.1 fusion.53
  314.4 1.6 fusion.39
  316.0 0.7 fusion.82
  316.7 1.6 fusion.38
  318.3 0.7 fusion.80
  319.0 0.7 fusion.41
  319.7 0.7 fusion.40
  320.4 0.1 pad_maximum_fusion.1
  320.5 0.6 copy.36
  321.1 27.8 %all_to_all.62 = f32[2,32,16,256]{3,2,0,1:T(8,128)S(1)} all-to-all(f32[2,32,16,256]{3,2,0,1:T(8,128)S(1)} %copy.36), channel_id=1, replica_groups=mesh['px'=4,'pz'=8] {'px'}, dimensions={1} | all-to-all | bytes 2097152 | tf_op jit(solution)/shard_map/all_to_all | solution.py:46
  349.0 0.1 fusion.198
  349.1 0.5 fusion.78
  349.6 0.5 fusion.76
  350.0 0.5 fusion.45
  350.5 0.5 fusion.44
  351.0 0.3 copy.38
  351.3 12.4 %all_to_all.63 = f32[2,8,32,256]{3,1,0,2:T(8,128)S(1)} all-to-all(f32[2,8,32,256]{3,1,0,2:T(8,128)S(1)} %copy.38), channel_id=1, replica_groups=mesh['px'=4,'pz'=8] {'pz'}, dimensions={2} | all-to-all | bytes 1048576 | tf_op jit(solution)/shard_map/all_to_all | solution.py:51
  363.9 35.3 %fusion.6 = f32[8,4,1024]{2,0,1:T(8,128)S(1)} fusion(f32[8,4,2048]{2,0,1:T(8,128)S(1)} %bitcast.140), kind=kOutput, calls=%fused_computation.14 | convolution fusion | flops 834666496 | bytes 393216 | tf_op jit(solution)/shard_map/xyk,kz->xyz/dot_general | solution.py:56
  399.2 35.3 %fusion.49 = f32[8,4,1024]{2,0,1:T(8,128)S(1)} fusion(f32[8,4,1024]{2,0,1:T(8,128)S(1)} %fusion.6, f32[8,4,2048]{2,0,1:T(8,128)S(1)} %bitcast.139), kind=kOutput, calls=%fused_computation.55 | convolution fusion | flops 834732032 | bytes 524288 | tf_op jit(solution)/shard_map/xyk,kz->xyz/dot_general | solution.py:55
  434.6 0.1 copy.40
  434.6 0.7 reshape.25
  435.4 59.4 %all-gather.2.cloned.1.call-done = f32[8192,128]{1,0:T(8,128)} async-done(((f32[256,128]{1,0:T(8,128)}), f32[8192,128]{1,0:T(8,128)}) %all-gather.2.cloned.1.call-update) | async-done | bytes 4194320 | tf_op jit(solution)/shard_map/all_gather | solution.py:75
  494.8 3.5 gather_fusion
  (13 shorter events, 0.4 us)
Async XLA Ops:
  6.5 148.9 %reduce-scatter.2.cloned.1.call-start = ((), (), s32[]{:S(2)}) async-start(), calls=%async_computation.5 | async-start | bytes 4325376 | tf_op jit(solution)/shard_map/reduce_scatter | solution.py:71
  11.9 482.9 %all-gather.2.cloned.1.call-start = ((), (), s32[]{:S(2)}) async-start(), calls=%async_computation.6 | async-start | bytes 4325376 | tf_op jit(solution)/shard_map/all_gather | solution.py:75
  280.3 34.0 %copy-start = (f32[64,16,256]{2,1,0:T(8,128)S(1)}, f32[64,16,256]{2,1,0:T(8,128)}, u32[]{:S(2)}) copy-start(f32[64,16,256]{2,1,0:T(8,128)} %param.7) | copy-start | bytes 3145732
Sparse Core Ops, SparseCore 0:
  12.0 143.3 reduce-scatter.1
  435.5 59.2 all-gather.1
where the time goes:
time: 515 us; the launch traced here: 506 us
  waiting for transfers between devices  203 us (39%)
  matrix products  155 us (30%)
  blocking collectives  80.8 us (16%)
  local copies, waits for them, and re-layouts  44.9 us (9%)
  between operations  14.2 us (3%)
  other arithmetic  7.46 us (1%)
    reduce_scatter x1, waiting for transfers between devices, local(): lax.psum_scatter(dense, ('px', 'pz'), scatter_dimension=0, tiled=True)  144 us
    all_gather x1, waiting for transfers between devices, local(): whole = lax.all_gather(phi_blocks, ('px', 'pz'), axis=0, tiled=True)  59.4 us
    dot_general x1, matrix products, solve_field(): jnp.einsum('xyz,zk->xyk', field, sine, precision=lax.Precision.HIGHEST)  36.1 us
    dot_general x1, matrix products, solve_field(): jnp.einsum('xyz,zk->xyk', field, cosine, precision=lax.Precision.HIGHEST)  35.7 us
    dot_general x1, matrix products, solve_field(): jnp.einsum('xyk,kz->xyz', turned[0], cosine, precision=lax.Precision.HIGH...  35.3 us
    dot_general x1, matrix products, solve_field(): jnp.einsum('xyk,kz->xyz', turned[1], sine, precision=lax.Precision.HIGHEST)  35.3 us
    all_to_all x1, blocking collectives, solve_field(): lax.all_to_all(jnp.stack((real_part, imag_part)), 'px', split_axis=2, con...  27.9 us
    all_to_all x1, blocking collectives, solve_field(): lax.all_to_all(jnp.stack((real_part, imag_part)), 'px', split_axis=1, con...  27.8 us
  transfers between devices with their start and end apart: 2, of which 2 were waited for; matrix products, arithmetic and copies ran while one was open for 0% of the time, Pallas kernels for 0%

commit v1 on v0

v1 whole, which is shorter than its diff:
```python
import math

import jax
import jax.numpy as jnp
import numpy as np
from jax import lax
from jax.sharding import PartitionSpec as P

CXP = 8
CYP = 4
NZP = 1024
AXES = ("px", "pz")


def split_table(table):
    high = table.astype(np.float32).astype(jnp.bfloat16)
    low = (table - high.astype(np.float64)).astype(np.float32).astype(jnp.bfloat16)
    return np.asarray(high), np.asarray(low)


def long_table():
    n = np.arange(NZP)[:, None]
    k = np.arange(2 * NZP)[None, :]
    angle = (n * k % (2 * NZP)) * (2.0 * math.pi / (2 * NZP))
    return np.cos(angle) + np.sin(angle)


def short_tables(wide, frequencies):
    period = 2 * wide
    folded = np.minimum(frequencies, period - frequencies)
    angle = (frequencies[:, None] * np.arange(wide)[None, :] % period) * (2.0 * math.pi / period)
    table = np.concatenate((np.cos(angle), np.sin(angle)), axis=0)
    weight = np.where((folded == 0) | (folded == wide), 1.0, 2.0) / period
    count = np.array([(folded == f).sum() for f in folded])
    weight = np.tile(weight / count, 2)
    return table, table * weight[:, None]


def split(values):
    high = lax.reduce_precision(values, 8, 7)
    return high.astype(jnp.bfloat16), (values - high).astype(jnp.bfloat16)


def product(form, values, table):
    high, low = split(values)
    t_high, t_low = table
    dot = lambda a, b: jnp.einsum(form, a, b, preferred_element_type=jnp.float32)
    return dot(high, t_high) + (dot(low, t_high) + dot(high, t_low))


def pick(form, one_hot, values):
    high, low = split(values)
    dot = lambda b: jnp.einsum(form, one_hot, b, preferred_element_type=jnp.float32)
    return dot(high) + dot(low)


def kept_frequencies(wide_y, n_px):
    own = 2 * wide_y // n_px
    return (np.arange(n_px)[:, None] * own + np.arange(own // 2 + 1)[None, :]).reshape(-1)


def local(charge, dest, local_ids, green_hat):
    n_px = lax.axis_size("px")
    n_pz = lax.axis_size("pz")
    n_dev = n_px * n_pz
    wide_x, wide_y = CXP * n_px, CYP * n_pz
    slots = charge.shape[0]
    cap = 2 * slots // n_dev
    pencil_blocks = CXP * CYP * NZP // 128
    own = 2 * wide_y // n_px
    group = 2 * NZP // n_dev

    green = lax.all_to_all(
        green_hat[: wide_x + 1, : own // 2 + 1], "px", split_axis=2, concat_axis=1, tiled=True
    )

    route = dest[:, 0]
    named = (route[:, None] == jnp.arange(n_dev)[None, :]).astype(jnp.bfloat16)
    before = jnp.asarray(np.tril(np.ones((slots, slots)), -1), jnp.bfloat16)
    rank = jnp.sum(
        jnp.einsum("st,td->sd", before, named, preferred_element_type=jnp.float32) * named, axis=1
    ).astype(jnp.int32)
    place = route * cap + rank
    packing = (place[:, None] == jnp.arange(n_dev * cap)[None, :]).astype(jnp.bfloat16)
    sent = pick("sr,sl->rl", packing, charge).reshape(n_dev, cap, 128)
    ids = jnp.einsum(
        "sr,s->r", packing, (local_ids + 1).astype(jnp.bfloat16), preferred_element_type=jnp.float32
    ).reshape(n_dev, 1, cap)
    sent = jnp.concatenate((sent, jnp.pad(ids, ((0, 0), (0, 0), (0, 128 - cap)))), axis=1)
    got = lax.all_to_all(sent, AXES, split_axis=0, concat_axis=0, tiled=True)
    ids = got[:, cap, :cap].reshape(n_dev * cap).astype(jnp.int32) - 1
    placing = (ids[:, None] == jnp.arange(pencil_blocks)[None, :]).astype(jnp.bfloat16)
    field = pick("rb,rl->bl", placing, got[:, :cap].reshape(n_dev * cap, 128))
    field = field.reshape(CXP * CYP, NZP)

    long = split_table(long_table())
    spectrum = product("pz,zk->pk", field, long)
    spectrum = spectrum.reshape(CXP * CYP, n_pz, n_px, group).transpose(2, 1, 0, 3)
    spectrum = spectrum.reshape(n_dev, CXP * CYP, group)
    turned = lax.all_to_all(spectrum, AXES, split_axis=0, concat_axis=0, tiled=True)
    planes = turned.reshape(n_px, n_pz, CXP, CYP, group).transpose(0, 2, 1, 3, 4)
    planes = planes.reshape(wide_x, wide_y, group)

    kept_y = kept_frequencies(wide_y, n_px)
    y_table, y_back = short_tables(wide_y, kept_y)
    x_table, x_back = short_tables(wide_x, np.arange(wide_x + 1))
    planes = product("xyk,qy->xqk", planes, split_table(y_table))
    planes = product("xqk,ux->uqk", planes, split_table(x_table))
    count_x, count_y = wide_x + 1, len(kept_y)
    planes = planes.reshape(2, count_x, 2, count_y, group) * green[None, :, None]
    planes = planes.reshape(2 * count_x, 2 * count_y, group)
    planes = product("uqk,ux->xqk", planes, split_table(x_back))
    planes = product("xqk,qy->xyk", planes, split_table(y_back))

    planes = planes.reshape(n_px, CXP, n_pz, CYP, group).transpose(0, 2, 1, 3, 4)
    planes = planes.reshape(n_dev, CXP * CYP, group)
    turned = lax.all_to_all(planes, AXES, split_axis=0, concat_axis=0, tiled=True)
    spectrum = turned.reshape(n_px, n_pz, CXP * CYP, group).transpose(2, 1, 0, 3)
    spectrum = spectrum.reshape(CXP * CYP, 2 * NZP)
    phi = product("pk,zk->pz", spectrum, long) * (1.0 / (2 * NZP))
    back = pick("rb,bl->rl", placing, phi.reshape(pencil_blocks, 128)).reshape(n_dev, cap, 128)
    got = lax.all_to_all(back, AXES, split_axis=0, concat_axis=0, tiled=True)
    return pick("sr,rl->sl", packing, got.reshape(n_dev * cap, 128))


def solution(mesh):
    return jax.shard_map(
        local,
        mesh=mesh,
        in_specs=(
            P(AXES, None),
            P(AXES, None),
            P(AXES),
            P(None, "px", "pz"),
        ),
        out_specs=P(AXES, None),
        check_vma=False,
    )
```

time: 515 us -> 123 us (0.24); the launches traced: 506 us -> 122 us
  waiting for transfers between devices: 203 us -> 11.9 us
  matrix products: 155 us -> 27.3 us
  blocking collectives: 80.8 us -> 27.5 us
  local copies, waits for them, and re-layouts: 44.9 us -> 28.1 us
  starting transfers between devices: 0.04 us -> 15.4 us
  between operations: 14.2 us -> 0.47 us
    reduce_scatter x1 -> x0, waiting for transfers between devices: 144 us -> none  [local(): lax.psum_scatter(dense, ('px', 'pz'), scatter_dimension=0, tiled=True)]
    dot_general x20 -> x28, matrix products: 155 us -> 27.3 us  [the longest x18 20.7 us: product(): jnp.einsum(form, a, b, preferred_element_type=jnp.float32)]
    all_gather x1 -> x0, waiting for transfers between devices: 59.4 us -> none  [local(): whole = lax.all_gather(phi_blocks, ('px', 'pz'), axis=0, tiled=True)]
    all_to_all x4 -> x2, blocking collectives: 80.8 us -> 27.5 us  [the longest x1 14.7 us: local(): lax.all_to_all(planes, AXES, split_axis=0, concat_axis=0, tiled=True)]
    unnamed x4 -> x33, local copies, waits for them, and re-layouts: 24.5 us -> 8.83 us
    all_to_all x0 -> x3, starting transfers between devices: none -> 15.4 us  [the longest x1 7.3 us: local(): got = lax.all_to_all(sent, AXES, split_axis=0, concat_axis=0, tiled=True)]
    all_to_all x0 -> x3, waiting for transfers between devices: none -> 11.9 us  [the longest x1 10 us: local(): got = lax.all_to_all(sent, AXES, split_axis=0, concat_axis=0, tiled=True)]
    dot_general x0 -> x3, local copies, waits for them, and re-layouts: none -> 9.76 us  [product(): jnp.einsum(form, a, b, preferred_element_type=jnp.float32)]
  transfers between devices with their start and end apart: 2 -> 3, of which waited for: 2 -> 3; matrix products, arithmetic and copies ran while one was open for 0% -> 16% of each run, Pallas kernels for 0% -> 0%
where the time goes in v1:
time: 123 us; the launch traced here: 122 us
  local copies, waits for them, and re-layouts  28.1 us (23%)
  blocking collectives  27.5 us (22%)
  matrix products  27.3 us (22%)
  starting transfers between devices  15.4 us (13%)
  waiting for transfers between devices  11.9 us (10%)
  other arithmetic  11.2 us (9%)
    dot_general x18, matrix products, product(): jnp.einsum(form, a, b, preferred_element_type=jnp.float32)  20.7 us
    all_to_all x1, blocking collectives, local(): lax.all_to_all(planes, AXES, split_axis=0, concat_axis=0, tiled=True)  14.7 us
    all_to_all x1, blocking collectives, local(): got = lax.all_to_all(back, AXES, split_axis=0, concat_axis=0, tiled=True)  12.8 us
    all_to_all x1, waiting for transfers between devices, local(): got = lax.all_to_all(sent, AXES, split_axis=0, concat_axis=0, tiled=True)  10 us
    dot_general x3, local copies, waits for them, and re-layouts, product(): jnp.einsum(form, a, b, preferred_element_type=jnp.float32)  9.76 us
    unnamed x33, local copies, waits for them, and re-layouts  8.83 us
    all_to_all x1, starting transfers between devices, local(): got = lax.all_to_all(sent, AXES, split_axis=0, concat_axis=0, tiled=True)  7.3 us
    dot_general x8, matrix products, pick(): jnp.einsum(form, one_hot, b, preferred_element_type=jnp.float32)  5.23 us
  transfers between devices with their start and end apart: 3, of which 3 were waited for; matrix products, arithmetic and copies ran while one was open for 16% of the time, Pallas kernels for 0%

profile of v1, /device:TPU:0, one launch (start us, length us, event | category | flops | bytes accessed | tf_op | source)
XLA Modules:
  0.0 121.9 jit_solution(8737284582628631513)
XLA Ops:
  0.0 0.8 add_convert_fusion
  0.8 1.1 fusion.11
  1.9 0.7 multiply_add_fusion
  2.9 1.3 %fusion.26 = f32[512,128]{1,0:T(8,128)S(1)} fusion(s32[256]{0:T(256)S(1)} %bitcast.91, f32[256,128]{1,0:T(8,128)} %param.23), kind=kOutput, calls=%fused_computation.48 | convolution fusion | flops 33751040 | bytes 394240 | tf_op jit(solution)/shard_map/sr,sl->rl/dot_general | solution.py:53
  4.3 1.3 %convolution_add_fusion.5 = f32[512,128]{1,0:T(8,128)S(1)} fusion(f32[512,128]{1,0:T(8,128)S(1)} %fusion.26, s32[256]{0:T(256)S(1)} %bitcast.92, f32[256,128]{1,0:T(8,128)} %param.23), kind=kOutput, calls=%fused_computation.21 | convolution fusion | flops 33849344 | bytes 656384 | tf_op jit(solution)/shard_map/sr,sl->rl/dot_general | solution.py:53
  5.6 0.8 pad_maximum_fusion
  6.4 7.3 %all-to-all-start = ((f32[32,17,128]{2,1,0:T(8,128)}), f32[32,17,128]{2,1,0:T(8,128)S(1)}, u32[]{:S(2)}, u32[]{:S(2)}) async-start(f32[32,17,128]{2,1,0:T(8,128)} %pad_maximum_fusion), calls=%async_computation | async-start | bytes 786432 | tf_op jit(solution)/shard_map/all_to_all | solution.py:90
  13.8 1.4 %copy.138 = f32[33,9,256]{0,1,2:T(8,128)S(1)} copy(f32[33,9,256]{2,1,0:T(8,128)S(1)} %slice.11) | data formatting | bytes 608256
  15.2 1.7 %reshape.99 = f32[4,1,19008]{2,1,0:T(1,128)} reshape(f32[256,9,33]{2,1,0:T(8,128)S(1)} %bitcast.77) | data formatting | bytes 608256
  16.9 10.0 %all-to-all-done = f32[32,17,128]{2,1,0:T(8,128)S(1)} async-done(((f32[32,17,128]{2,1,0:T(8,128)}), f32[32,17,128]{2,1,0:T(8,128)S(1)}, u32[]{:S(2)}, u32[]{:S(2)}) %all-to-all-start) | async-done | bytes 278560 | tf_op jit(solution)/shard_map/all_to_all | solution.py:90
  26.9 3.5 %all-to-all-start.2 = ((f32[4,1,19008]{2,1,0:T(1,128)}), f32[4,1,19008]{2,1,0:T(1,128)S(1)}, u32[]{:S(2)}, u32[]{:S(2)}) async-start(f32[4,1,19008]{2,1,0:T(1,128)} %reshape.99), calls=%async_computation.2 | async-start | bytes 610304 | tf_op jit(solution)/shard_map/all_to_all | solution.py:73
  31.4 3.2 %fusion.56 = f32[32,2048]{1,0:T(8,128)S(1)} fusion(bf16[1024,2048]{1,0:T(8,128)(2,1)} %constant.36.clone, f32[32,1024]{1,0:T(8,128)S(1)} %reshape.70), kind=kOutput, calls=%fused_computation.87 | convolution fusion | flops 134316032 | bytes 4587520 | tf_op jit(solution)/shard_map/pz,zk->pk/dot_general | solution.py:47
  34.9 0.8 fusion.60
  35.7 1.4 %copy-done.2 = bf16[1024,2048]{1,0:T(8,128)(2,1)S(1)} copy-done((bf16[1024,2048]{1,0:T(8,128)(2,1)S(1)}, bf16[1024,2048]{1,0:T(8,128)(2,1)}, u32[]{:S(2)}) %copy-start.2) | copy-done | bytes 4194328
  37.1 0.8 fusion
  38.6 1.0 reshape.101
  39.6 0.5 all-to-all-done.2
  40.1 4.7 %all-to-all-start.1 = ((f32[32,1,2048]{2,1,0:T(1,128)}), f32[32,1,2048]{2,1,0:T(1,128)S(1)}, u32[]{:S(2)}, u32[]{:S(2)}) async-start(f32[32,1,2048]{2,1,0:T(1,128)} %reshape.101), calls=%async_computation.1 | async-start | bytes 524288 | tf_op jit(solution)/shard_map/all_to_all | solution.py:100
  44.8 0.5 broadcast.18
  45.3 1.5 %reduce.4 = f32[4,19008]{1,0:T(4,128)S(1)} reduce(f32[4,1,19008]{2,1,0:T(1,128)S(1)} %all-to-all-done.2, f32[]{:T(128)} %broadcast.18), dimensions={1}, to_apply=%all_to_all.25.reduce_sub_computation | reduce | bytes 608260 | tf_op jit(solution)/shard_map/all_to_all | solution.py:73
  46.8 0.7 reshape.100
  47.5 1.3 %copy.137 = f32[33,9,4,64]{3,2,0,1:T(4,128)S(1)} copy(f32[33,9,4,64]{0,1,3,2:T(8,128)S(1)} %bitcast.78) | data formatting | bytes 608256 | tf_op jit(solution)/shard_map/all_to_all | solution.py:73
  49.1 1.5 %mul.34 = f32[66,72,64]{2,1,0:T(8,128)} reshape(f32[2,33,2,36,64]{4,3,2,1,0:T(8,128)S(1)} %mul.33) | data formatting | bytes 2433024 | tf_op jit(solution)/shard_map/mul | solution.py:110
  50.7 3.1 %copy.127 = f32[66,72,64]{1,2,0:T(8,128)} copy(f32[66,72,64]{2,1,0:T(8,128)} %mul.34) | data formatting | bytes 2433024 | tf_op jit(solution)/shard_map/mul | solution.py:110
  53.7 1.4 %all-to-all-done.1 = f32[32,1,2048]{2,1,0:T(1,128)S(1)} async-done(((f32[32,1,2048]{2,1,0:T(1,128)}), f32[32,1,2048]{2,1,0:T(1,128)S(1)}, u32[]{:S(2)}, u32[]{:S(2)}) %all-to-all-start.1) | async-done | bytes 262176 | tf_op jit(solution)/shard_map/all_to_all | solution.py:100
  55.2 1.3 %reduce.5 = f32[32,2048]{1,0:T(8,128)S(1)} reduce(f32[32,1,2048]{2,1,0:T(1,128)S(1)} %all-to-all-done.1, f32[]{:T(128)} %broadcast.18), dimensions={1}, to_apply=%all_to_all.24.reduce_sub_computation | reduce | bytes 524292 | tf_op jit(solution)/shard_map/all_to_all | solution.py:100
  58.8 0.9 fusion.20
  59.6 2.9 %copy.120 = f32[72,64,66]{0,1,2:T(8,128)} copy(f32[72,64,66]{2,0,1:T(8,128)S(1)} %fusion.20) | data formatting | bytes 2433024 | tf_op jit(solution)/shard_map/xqk,ux->uqk/dot_general | solution.py:47
  62.5 0.9 fusion.32
  63.4 2.3 %fusion.30 = f32[72,64,66]{2,0,1:T(8,128)} fusion(bf16[66,32,1]{0,1,2:T(8,128)(2,1)S(1)} %copy-done.11, bf16[32,72,64]{1,2,0:T(8,128)(2,1)S(1)} %get-tuple-element.10), kind=kOutput, calls=%fused_computation.52 | convolution fusion | flops 19464192 | bytes 1515648 | tf_op jit(solution)/shard_map/xqk,ux->uqk/dot_general | solution.py:47
  65.7 3.9 %copy.121 = f32[72,64,66]{0,1,2:T(8,128)} copy(f32[72,64,66]{2,0,1:T(8,128)} %fusion.30) | data formatting | bytes 2433024 | tf_op jit(solution)/shard_map/xqk,ux->uqk/dot_general | solution.py:47
  69.7 2.9 %copy.122 = f32[72,64,66]{0,1,2:T(8,128)} copy(f32[72,64,66]{2,0,1:T(8,128)S(1)} %fusion.32) | data formatting | bytes 2433024 | tf_op jit(solution)/shard_map/xqk,ux->uqk/dot_general | solution.py:47
  72.6 4.6 %fusion.1 = (bf16[66,72,64]{1,2,0:T(8,128)(2,1)S(1)}, f32[66,72,64]{1,2,0:T(8,128)S(1)}) fusion(f32[66,72,64]{1,2,0:T(8,128)} %copy.127, f32[72,64,66]{0,1,2:T(8,128)} %copy.122, f32[72,64,66]{0,1,2:T(8,128)} %copy.120, f32[72,64,66]{0,1,2:T(8,128)} %copy.121), kind=kLoop, calls=%fused_computation.4 | loop fusion | flops 1824768 | bytes 6690816 | tf_op jit(solution)/shard_map/convert_element_type | solution.py:41
  77.4 0.5 copy-done.6
  77.9 0.8 fusion.7
  78.7 0.8 fusion.13
  79.5 0.9 fusion.16
  80.5 0.6 fusion.18
  81.1 0.6 fusion.28
  81.7 0.6 fusion.6
  83.0 14.7 %all_to_all.35 = f32[32,1,2048]{2,1,0:T(1,128)S(1)} all-to-all(f32[32,1,2048]{2,1,0:T(1,128)S(1)} %reshape.103), channel_id=1, replica_groups=mesh['px'=4,'pz'=8] {'px','pz'}, dimensions={0} | all-to-all | bytes 524288 | tf_op jit(solution)/shard_map/all_to_all | solution.py:117
  97.7 1.3 %reduce.6 = f32[32,2048]{1,0:T(8,128)S(1)} reduce(f32[32,1,2048]{2,1,0:T(1,128)S(1)} %all_to_all.35, f32[]{:T(128)} %broadcast.18), dimensions={1}, to_apply=%all_to_all.28.reduce_sub_computation | reduce | bytes 524292 | tf_op jit(solution)/shard_map/all_to_all | solution.py:117
  99.9 3.7 %fusion.51 = f32[32,1024]{1,0:T(8,128)S(1)} fusion(bf16[1024,2048]{1,0:T(8,128)(2,1)} %constant.36.clone, f32[32,2048]{1,0:T(8,128)S(1)} %reshape.78), kind=kOutput, calls=%fused_computation.85 | convolution fusion | flops 134414336 | bytes 4587520 | tf_op jit(solution)/shard_map/pk,zk->pz/dot_general | solution.py:47
  103.7 1.3 %fusion.58 = f32[32,1024]{1,0:T(8,128)S(1)} fusion(bf16[1024,2048]{1,0:T(8,128)(2,1)S(1)} %copy-done.1, f32[32,2048]{1,0:T(8,128)S(1)} %reshape.78), kind=kOutput, calls=%fused_computation.88 | convolution fusion | flops 134348800 | bytes 4587520 | tf_op jit(solution)/shard_map/pk,zk->pz/dot_general | solution.py:47
  105.0 0.8 copy-done.3
  105.8 1.3 %fusion.10 = f32[32,1024]{1,0:T(8,128)S(1)} fusion(f32[32,1024]{1,0:T(8,128)S(1)} %fusion.58, f32[32,1024]{1,0:T(8,128)S(1)} %fusion.51, bf16[1024,2048]{1,0:T(8,128)(2,1)S(1)} %copy-done.3, f32[32,2048]{1,0:T(8,128)S(1)} %reshape.78), kind=kOutput, calls=%fused_computation.24 | convolution fusion | flops 134447104 | bytes 4849664 | tf_op jit(solution)/shard_map/pk,zk->pz/dot_general | solution.py:47
  107.8 12.8 %all_to_all.36 = f32[32,16,128]{2,1,0:T(8,128)S(1)} all-to-all(f32[32,16,128]{2,1,0:T(8,128)S(1)} %bitcast.88), channel_id=1, replica_groups=mesh['px'=4,'pz'=8] {'px','pz'}, dimensions={0} | all-to-all | bytes 524288 | tf_op jit(solution)/shard_map/all_to_all | solution.py:122
  120.9 0.9 convolution_add_fusion.7
  (59 shorter events, 7.8 us)
Async XLA Ops:
  0.0 13.7 %copy-start.4 = (f32[64,16,256]{2,1,0:T(8,128)S(1)}, f32[64,16,256]{2,1,0:T(8,128)}, u32[]{:S(2)}) copy-start(f32[64,16,256]{2,1,0:T(8,128)} %param.26) | copy-start | bytes 3145732
  6.4 20.5 %all-to-all-start = ((f32[32,17,128]{2,1,0:T(8,128)}), f32[32,17,128]{2,1,0:T(8,128)S(1)}, u32[]{:S(2)}, u32[]{:S(2)}) async-start(f32[32,17,128]{2,1,0:T(8,128)} %pad_maximum_fusion), calls=%async_computation | async-start | bytes 786432 | tf_op jit(solution)/shard_map/all_to_all | solution.py:90
  26.9 13.2 %all-to-all-start.2 = ((f32[4,1,19008]{2,1,0:T(1,128)}), f32[4,1,19008]{2,1,0:T(1,128)S(1)}, u32[]{:S(2)}, u32[]{:S(2)}) async-start(f32[4,1,19008]{2,1,0:T(1,128)} %reshape.99), calls=%async_computation.2 | async-start | bytes 610304 | tf_op jit(solution)/shard_map/all_to_all | solution.py:73
  31.4 3.5 %copy-start = (bf16[1024,2048]{1,0:T(8,128)(2,1)S(1)}, bf16[1024,2048]{1,0:T(8,128)(2,1)}, u32[]{:S(2)}) copy-start(bf16[1024,2048]{1,0:T(8,128)(2,1)} %constant.36.clone) | copy-start | bytes 12582916
  34.9 2.2 %copy-start.2 = (bf16[1024,2048]{1,0:T(8,128)(2,1)S(1)}, bf16[1024,2048]{1,0:T(8,128)(2,1)}, u32[]{:S(2)}) copy-start(bf16[1024,2048]{1,0:T(8,128)(2,1)} %constant.37.clone) | copy-start | bytes 12582916
  40.1 15.1 %all-to-all-start.1 = ((f32[32,1,2048]{2,1,0:T(1,128)}), f32[32,1,2048]{2,1,0:T(1,128)S(1)}, u32[]{:S(2)}, u32[]{:S(2)}) async-start(f32[32,1,2048]{2,1,0:T(1,128)} %reshape.101), calls=%async_computation.1 | async-start | bytes 524288 | tf_op jit(solution)/shard_map/all_to_all | solution.py:100
  53.7 3.6 %copy-start.8 = (bf16[72,32,1]{0,1,2:T(8,128)(2,1)S(1)}, bf16[72,32,1]{0,1,2:T(8,128)(2,1)}, u32[]{:S(2)}) copy-start(bf16[72,32,1]{0,1,2:T(8,128)(2,1)} %constant.48) | copy-start | bytes 13828
  57.0 1.1 copy-start.12
  58.1 0.7 copy-start.7
  62.5 0.9 copy-start.11
  77.2 0.7 copy-start.6
  77.9 1.6 %copy-start.10 = (bf16[66,32,1]{0,1,2:T(8,128)(2,1)S(1)}, bf16[66,32,1]{0,1,2:T(8,128)(2,1)}, u32[]{:S(2)}) copy-start(bf16[66,32,1]{0,1,2:T(8,128)(2,1)} %constant.53) | copy-start | bytes 12676
  79.5 1.0 copy-start.5
  79.5 2.2 %copy-start.9 = (bf16[72,32,1]{0,1,2:T(8,128)(2,1)S(1)}, bf16[72,32,1]{0,1,2:T(8,128)(2,1)}, u32[]{:S(2)}) copy-start(bf16[72,32,1]{0,1,2:T(8,128)(2,1)} %constant.55) | copy-start | bytes 13828
  99.9 3.7 %copy-start.1 = (bf16[1024,2048]{1,0:T(8,128)(2,1)S(1)}, bf16[1024,2048]{1,0:T(8,128)(2,1)}, u32[]{:S(2)}) copy-start(bf16[1024,2048]{1,0:T(8,128)(2,1)} %constant.36.clone) | copy-start | bytes 12582916
  103.6 2.2 %copy-start.3 = (bf16[1024,2048]{1,0:T(8,128)(2,1)S(1)}, bf16[1024,2048]{1,0:T(8,128)(2,1)}, u32[]{:S(2)}) copy-start(bf16[1024,2048]{1,0:T(8,128)(2,1)} %constant.37.clone) | copy-start | bytes 12582916

commit v2 on v1

--- a/solution.py
+++ b/solution.py
@@ -1,9 +1,12 @@
+import functools
 import math
 
 import jax
 import jax.numpy as jnp
 import numpy as np
 from jax import lax
+from jax.experimental import pallas as pl
+from jax.experimental.pallas import tpu as pltpu
 from jax.sharding import PartitionSpec as P
 
 CXP = 8
@@ -123,9 +126,338 @@
     return pick("sr,rl->sl", packing, got.reshape(n_dev * cap, 128))
 
 
+LANES = 128
+GROUP = 64
+KEPT = 8
+HALF = 32
+WIDE = 32
+MESH = pl.DeviceIdType.MESH
+
+
+def unit_rows(frequencies, is_sine, wide):
+    period = 2 * wide
+    angle = (frequencies[:, None] * np.arange(wide)[None, :] % period) * (2.0 * math.pi / period)
+    weight = np.where((frequencies == 0) | (frequencies == wide), 1.0, 2.0) / period
+    return np.where(is_sine[:, None], np.sin(angle), np.cos(angle)) * np.sqrt(weight)[:, None]
+
+
+def plane_tables(n_px, n_pz):
+    starts = np.array([0, 16, 33, 49])
+    raw = (starts[:, None] + np.arange(KEPT)[None, :]).reshape(-1)
+    folded = np.minimum(raw, 2 * WIDE - raw)
+    frequencies = np.concatenate((folded, np.where(folded == 0, WIDE, folded)))
+    sine = np.concatenate((np.zeros(HALF, bool), folded != 0))
+    rows = unit_rows(frequencies, sine, WIDE).reshape(2 * n_px, KEPT, n_pz, CYP)
+    eye_i, eye_a = np.eye(n_px), np.eye(4)
+    y_table = np.einsum("gqjb,iI,aA->ijabgIqA", rows, eye_i, eye_a)
+    y_table = y_table.reshape(n_px * n_pz * 16, 2 * n_px * n_px * KEPT * 4)
+    base = np.arange(HALF)
+    frequencies = np.concatenate((base, np.where(base == 0, WIDE, base)))
+    sine = np.concatenate((np.zeros(HALF, bool), base != 0))
+    rows = unit_rows(frequencies, sine, WIDE).reshape(2 * HALF, n_px, 2, 4)
+    x_table = np.einsum("uiha,qQ->hiqauQ", rows, np.eye(KEPT))
+    x_table = x_table.reshape(2 * n_px * KEPT * 4, 2 * HALF * KEPT)
+    return y_table, x_table
+
+
+def halves(values):
+    high = values.astype(jnp.bfloat16)
+    return high, (values - high.astype(jnp.float32)).astype(jnp.bfloat16)
+
+
+def mm(a, b, contract=((1,), (0,))):
+    return lax.dot_general(a, b, (contract, ((), ())), preferred_element_type=jnp.float32)
+
+
+def mm_left(values, high, low, contract=((1,), (0,))):
+    v_high, v_low = halves(values)
+    rows = values.shape[0]
+    both = mm(jnp.concatenate((v_high, v_low), axis=0), high, contract)
+    return both[:rows] + (both[rows:] + mm(v_high, low, contract))
+
+
+def mm_pick(one_hot, values):
+    high, low = halves(values)
+    return mm(one_hot, high) + mm(one_hot, low)
+
+
+def iota(shape, axis):
+    return lax.broadcasted_iota(jnp.int32, shape, axis)
+
+
+def as_row(column):
+    return jnp.transpose(jnp.broadcast_to(column, (column.shape[0], LANES)))[0:1, :]
+
+
+def as_column(row):
+    return jnp.transpose(jnp.broadcast_to(row, (LANES, row.shape[1])))[:, 0:1]
+
+
+def one(mask):
+    return jnp.where(mask, 1.0, 0.0).astype(jnp.bfloat16)
+
+
+def fused(
+    n_px, n_pz, charge_ref, dest_ref, ids_ref, green_hbm, zh_hbm, zl_hbm, yh_hbm, yl_hbm, xh_hbm,
+    xl_hbm, out_ref, green, zh, zl, yh, yl, xh, xl, ids_send, ids_recv, charge_send, charge_recv,
+    green_send, green_recv, spec_send, spec_recv, back_send, back_recv, out_send, out_recv, scale,
+    load_sems, send_sems, recv_sems
+):
+    n_dev = n_px * n_pz
+    mi, mj = lax.axis_index("px"), lax.axis_index("pz")
+    me = mi * n_pz + mj
+    slots = charge_ref.shape[0]
+    cap = charge_send.shape[1]
+    rows = n_dev * cap
+    blocks = CXP * CYP * NZP // LANES
+
+    barrier = pltpu.get_barrier_semaphore()
+
+    def greet(step, carry):
+        peer = lax.rem(me + step, n_dev)
+        pl.semaphore_signal(
+            barrier, inc=1, device_id=(peer // n_pz, lax.rem(peer, n_pz)), device_id_type=MESH
+        )
+        return carry
+
+    lax.fori_loop(1, n_dev, greet, 0)
+
+    loads = [
+        pltpu.make_async_copy(source, target, load_sems.at[number])
+        for number, (source, target) in enumerate((
+            (green_hbm.at[pl.ds(0, 40)], green), (zh_hbm, zh), (zl_hbm, zl), (yh_hbm, yh),
+            (yl_hbm, yl), (xh_hbm, xh), (xl_hbm, xl),
+        ))
+    ]
+    for load in loads:
+        load.start()
+
+    def block_copy(send, recv, number, peer):
+        return pltpu.make_async_remote_copy(
+            src_ref=send.at[peer],
+            dst_ref=recv.at[me],
+            send_sem=send_sems.at[number],
+            recv_sem=recv_sems.at[number],
+            device_id=(peer // n_pz, lax.rem(peer, n_pz)),
+            device_id_type=MESH,
+        )
+
+    def send_all(send, recv, number):
+        def body(step, carry):
+            block_copy(send, recv, number, lax.rem(me + step, n_dev)).start()
+            return carry
+
+        lax.fori_loop(1, n_dev, body, 0)
+        recv[me] = send[me]
+
+    def all_of(send, recv, number, count):
+        return pltpu.make_async_remote_copy(
+            src_ref=send.at[pl.ds(0, count)],
+            dst_ref=recv.at[pl.ds(0, count)],
+            send_sem=send_sems.at[number],
+            recv_sem=recv_sems.at[number],
+            device_id=(mi, mj),
+            device_id_type=MESH,
+        )
+
+    dest = dest_ref[...]
+    named = one(dest == iota((slots, LANES), 1))
+    before = one(iota((slots, slots), 1) < iota((slots, slots), 0))
+    rank = jnp.sum(mm(before, named) * named.astype(jnp.float32), axis=1, keepdims=True)
+    place = dest.astype(jnp.float32) * cap + rank
+    ids = ids_ref[...].astype(jnp.float32) + 1.0
+    dest_row = as_row(dest.astype(jnp.float32))
+    owned = jnp.where(dest_row == iota((n_dev, slots), 0).astype(jnp.float32), ids, 0.0)
+    ranked = one(rank == iota((slots, LANES), 1).astype(jnp.float32))
+    ids_send[...] = mm(owned.astype(jnp.bfloat16), ranked).reshape(n_dev, 1, LANES)
+    packing = one(as_row(place) == iota((rows, slots), 0).astype(jnp.float32))
+    charge_send[...] = mm_pick(packing, charge_ref[...]).reshape(n_dev, cap, LANES)
+    pl.semaphore_wait(barrier, n_dev - 1)
+    send_all(ids_send, ids_recv, 0)
+    send_all(charge_send, charge_recv, 1)
+
+    loads[0].wait()
+    shifted = mi >= n_px // 2
+    kept = jnp.where(shifted, green[0:33, 1:9, :], green[0:33, 0:8, :])
+    wide = jnp.transpose(kept[0:HALF].reshape(HALF * KEPT, 256))
+    edge = green[0:40, 0, :]
+    edge = jnp.concatenate((kept[HALF], edge, jnp.zeros((LANES - 48, 256), jnp.float32)), axis=0)
+    green_send[...] = jnp.concatenate((wide, jnp.transpose(edge)), axis=1).reshape(n_px, GROUP, 384)
+
+    def green_copy(target):
+        return pltpu.make_async_remote_copy(
+            src_ref=green_send.at[target],
+            dst_ref=green_recv.at[mi],
+            send_sem=send_sems.at[2],
+            recv_sem=recv_sems.at[2],
+            device_id=(target, mj),
+            device_id_type=MESH,
+        )
+
+    for step in range(1, n_px):
+        green_copy(lax.rem(mi + step, n_px)).start()
+    green_recv[mi] = green_send[mi]
+
+    all_of(ids_send, ids_recv, 0, n_dev - 1).wait_recv()
+    line = iota((rows, n_dev), 0)
+    spread = mm(one(line // cap == iota((rows, n_dev), 1)), ids_recv[...].reshape(n_dev, LANES).astype(jnp.bfloat16))
+    own_lane = iota((rows, LANES), 1) == lax.rem(iota((rows, LANES), 0), cap)
+    ids = jnp.sum(jnp.where(own_lane, spread, 0.0), axis=1, keepdims=True)
+    lines = CXP * CYP
+
+    def target_of(index):
+        return (lax.rem(index, lines) * (NZP // LANES) + index // lines + 1).astype(jnp.float32)
+
+    taking = one(ids == target_of(iota((rows, blocks), 1)))
+    placing = one(as_row(ids) == target_of(iota((blocks, rows), 0)))
+    all_of(charge_send, charge_recv, 1, n_dev - 1).wait_recv()
+    field = mm_pick(placing, charge_recv[...].reshape(rows, LANES))
+    field = jnp.concatenate([field[lines * c : lines * (c + 1)] for c in range(NZP // LANES)], axis=1)
+
+    f_high, f_low = halves(field)
+    f_both = jnp.concatenate((f_high, f_low), axis=0)
+    loads[1].wait()
+    loads[2].wait()
+    first = iota((lines // 2, LANES), 1) < GROUP
+
+    def forward(step, carry):
+        j = lax.rem(mj + step, n_pz)
+        columns = pl.ds(pl.multiple_of(j * 256, 256), 256)
+        both = mm(f_both, zh[:, columns])
+        total = both[:lines] + (both[lines:] + mm(f_high, zl[:, columns]))
+        for pair in range(2):
+            tile = total[:, pair * LANES : (pair + 1) * LANES]
+            low, high = tile[: lines // 2], tile[lines // 2 :]
+            low_turned, high_turned = pltpu.roll(low, GROUP, 1), pltpu.roll(high, GROUP, 1)
+            spec_send[2 * pair * n_pz + j] = jnp.where(first, low, high_turned)
+            spec_send[(2 * pair + 1) * n_pz + j] = jnp.where(first, low_turned, high)
+        for turn in range(n_px):
+            peer = lax.rem(mi + turn, n_px) * n_pz + j
+
+            @pl.when(peer != me)
+            def _():
+                block_copy(spec_send, spec_recv, 3, peer).start()
+
+        return carry
+
+    lax.fori_loop(0, n_pz, forward, 0)
+    spec_recv[me] = spec_send[me]
+
+    all_of(green_send, green_recv, 2, n_px - 1).wait_recv()
+    lane = iota((GROUP, 256), 1)
+    source, target = iota((LANES, 512), 0), iota((LANES, 512), 1)
+    wanted = jnp.where(target == 256, HALF, lax.rem(target, 256) // KEPT) + KEPT
+    picking = one((source == wanted) & (lax.rem(target, KEPT) == 0))
+    e_high, e_low = halves(green_recv[2, :, 256:384])
+    e_rest = (green_recv[2, :, 256:384] - e_high.astype(jnp.float32) - e_low.astype(jnp.float32)).astype(jnp.bfloat16)
+    nyquist = mm(e_high, picking) + (mm(e_low, picking) + mm(e_rest, picking))
+    for i in range(n_px):
+        wide = green_recv[i, :, 0:256]
+        edge = jnp.concatenate((green_recv[i, :, 256:384], wide[:, LANES:]), axis=1)
+        full = jnp.concatenate((wide, jnp.where(lane < KEPT, edge, wide)), axis=1)
+        scale[i * GROUP : (i + 1) * GROUP, :] = full
+        if i == 0:
+            full = jnp.where(lax.rem(iota((GROUP, 512), 1), KEPT) == 0, nyquist, full)
+        scale[(n_px + i) * GROUP : (n_px + i + 1) * GROUP, :] = full
+
+    for load in loads[3:]:
+        load.wait()
+    all_of(spec_send, spec_recv, 3, n_dev - 1).wait_recv()
+    planes = jnp.transpose(spec_recv[...].reshape(n_dev * 16, LANES))
+    planes = mm_left(planes, yh[...], yl[...])
+    groups = 2 * n_px
+    planes = jnp.concatenate(
+        [
+            jnp.concatenate(
+                [planes[h * GROUP : (h + 1) * GROUP, g * LANES : (g + 1) * LANES] for h in range(2)], axis=1
+            )
+            for g in range(groups)
+        ],
+        axis=0,
+    )
+    planes = mm_left(planes, xh[...], xl[...]) * scale[...]
+    planes = mm_left(planes, xh[...], xl[...], ((1,), (1,)))
+    planes = jnp.concatenate(
+        [
+            jnp.concatenate(
+                [planes[g * GROUP : (g + 1) * GROUP, h * LANES : (h + 1) * LANES] for g in range(groups)], axis=1
+            )
+            for h in range(2)
+        ],
+        axis=0,
+    )
+    p_high, p_low = halves(planes)
+    right = ((1,), (1,))
+    planes = mm(yh[...], p_high, right) + (mm(yh[...], p_low, right) + mm(yl[...], p_high, right))
+    back_send[...] = planes.reshape(n_dev, 16, LANES)
+    send_all(back_send, back_recv, 4)
+
+    all_of(back_send, back_recv, 4, n_dev - 1).wait_recv()
+    pieces = []
+    for j in range(n_pz):
+        for pair in range(2):
+            left, other = back_recv[2 * pair * n_pz + j], back_recv[(2 * pair + 1) * n_pz + j]
+            low = jnp.where(first, left, pltpu.roll(other, GROUP, 1))
+            high = jnp.where(first, pltpu.roll(left, GROUP, 1), other)
+            pieces.append(jnp.concatenate((low, high), axis=0))
+    phi = mm_left(jnp.concatenate(pieces, axis=1), zh[...], zl[...], right)
+    phi = jnp.concatenate([phi[:, c * LANES : (c + 1) * LANES] for c in range(NZP // LANES)], axis=0)
+    out_send[...] = mm_pick(taking, phi).reshape(n_dev, cap, LANES)
+    send_all(out_send, out_recv, 5)
+    unpacking = one(place == iota((slots, rows), 1).astype(jnp.float32))
+    all_of(out_send, out_recv, 5, n_dev - 1).wait_recv()
+    out_ref[...] = mm_pick(unpacking, out_recv[...].reshape(rows, LANES))
+
+    all_of(ids_send, ids_recv, 0, n_dev - 1).wait_send()
+    all_of(charge_send, charge_recv, 1, n_dev - 1).wait_send()
+    all_of(green_send, green_recv, 2, n_px - 1).wait_send()
+    all_of(spec_send, spec_recv, 3, n_dev - 1).wait_send()
+    all_of(back_send, back_recv, 4, n_dev - 1).wait_send()
+    all_of(out_send, out_recv, 5, n_dev - 1).wait_send()
+
+
+def local_fused(charge, dest, local_ids, green_hat):
+    n_px, n_pz = lax.axis_size("px"), lax.axis_size("pz")
+    n_dev = n_px * n_pz
+    slots = charge.shape[0]
+    cap = 2 * slots // n_dev
+    y_table, x_table = plane_tables(n_px, n_pz)
+    tables = [
+        piece
+        for table in (long_table() / math.sqrt(2 * NZP), y_table, x_table)
+        for piece in split_table(table)
+    ]
+    exchange = lambda lead, rows: [pltpu.VMEM((lead, rows, LANES), jnp.float32)] * 2
+    vmem, anywhere = pl.BlockSpec(memory_space=pltpu.VMEM), pl.BlockSpec(memory_space=pl.ANY)
+    return pl.pallas_call(
+        functools.partial(fused, n_px, n_pz),
+        out_shape=jax.ShapeDtypeStruct(charge.shape, jnp.float32),
+        in_specs=[vmem] * 3 + [anywhere] * 7,
+        out_specs=vmem,
+        scratch_shapes=[
+            pltpu.VMEM((40,) + green_hat.shape[1:], jnp.float32),
+            *[pltpu.VMEM(table.shape, jnp.bfloat16) for table in tables],
+            *exchange(n_dev, 1),
+            *exchange(n_dev, cap),
+            *[pltpu.VMEM((n_px, GROUP, 384), jnp.float32)] * 2,
+            *exchange(n_dev, 16),
+            *exchange(n_dev, 16),
+            *exchange(n_dev, cap),
+            pltpu.VMEM((2 * n_px * GROUP, 2 * HALF * KEPT), jnp.float32),
+            pltpu.SemaphoreType.DMA((7,)),
+            pltpu.SemaphoreType.DMA((6,)),
+            pltpu.SemaphoreType.DMA((6,)),
+        ],
+        compiler_params=pltpu.CompilerParams(
+            collective_id=0, has_side_effects=True, vmem_limit_bytes=48 * 1024 * 1024
+        ),
+    )(charge, dest, local_ids.reshape(1, slots), green_hat, *tables)
+
+
 def solution(mesh):
+    planes = mesh.shape["px"] == 4 and mesh.shape["pz"] == 8
     return jax.shard_map(
-        local,
+        local_fused if planes else local,
         mesh=mesh,
         in_specs=(
             P(AXES, None),

time: 123 us -> 59.6 us (0.48)
  Pallas kernels: 0 us -> 50.1 us
  blocking collectives: 27.5 us -> 0 us
  matrix products: 27.3 us -> 0 us
  local copies, waits for them, and re-layouts: 28.1 us -> 8.61 us
  starting transfers between devices: 15.4 us -> 0 us
  waiting for transfers between devices: 11.9 us -> 0 us
  other arithmetic: 11.2 us -> 0 us
    pallas_call x0 -> x1, Pallas kernels: none -> 50.1 us  [local_fused(): pl.pallas_call(functools.partial(fused, n_px, n_pz), out_shape=jax.ShapeD...]
    all_to_all x2 -> x0, blocking collectives: 27.5 us -> none  [the longest x1 14.7 us: local(): lax.all_to_all(planes, AXES, split_axis=0, concat_axis=0, tiled=True)]
    dot_general x28 -> x0, matrix products: 27.3 us -> none  [the longest x18 20.7 us: product(): jnp.einsum(form, a, b, preferred_element_type=jnp.float32)]
    all_to_all x3 -> x0, starting transfers between devices: 15.4 us -> none  [the longest x1 7.3 us: local(): got = lax.all_to_all(sent, AXES, split_axis=0, concat_axis=0, tiled=True)]
    all_to_all x3 -> x0, waiting for transfers between devices: 11.9 us -> none  [the longest x1 10 us: local(): got = lax.all_to_all(sent, AXES, split_axis=0, concat_axis=0, tiled=True)]
    dot_general x3 -> x0, local copies, waits for them, and re-layouts: 9.76 us -> none  [product(): jnp.einsum(form, a, b, preferred_element_type=jnp.float32)]
    convert_element_type x6 -> x0, other arithmetic: 5.64 us -> none  [the longest x4 4.86 us: split(): return (high.astype(jnp.bfloat16), (values - high).astype(jnp.bfloat16))]
    mul x4 -> x0, local copies, waits for them, and re-layouts: 4.91 us -> none  [local(): planes.reshape(2, count_x, 2, count_y, group) * green[None, :, None]]
  transfers between devices with their start and end apart: 3 -> 0, of which waited for: 3 -> 0; matrix products, arithmetic and copies ran while one was open for 16% -> 0% of each run, Pallas kernels for 0% -> 0%
where the time goes in v2:
time: 59.6 us; the launch traced here: 58.8 us
  Pallas kernels  50.1 us (84%)
  local copies, waits for them, and re-layouts  8.61 us (14%)
    pallas_call x1, Pallas kernels, local_fused(): pl.pallas_call(functools.partial(fused, n_px, n_pz), out_shape=jax.ShapeD...  50.1 us
    unnamed x16, local copies, waits for them, and re-layouts  8.61 us

profile of v2, /device:TPU:0, one launch (start us, length us, event | category | flops | bytes accessed | tf_op | source)
XLA Modules:
  0.0 58.8 jit_solution(10105658185453748765)
XLA Ops:
  0.0 0.8 %copy.11.dest_ref = s32[256,1]{1,0:T(8,128)S(1)} copy(s32[256,1]{0,1:T(1,128)} %param.11) | data formatting | bytes 2048 | tf_op args[1]
  0.8 0.0 copy-start
  0.8 1.2 %copy-done = f32[64,16,256]{2,1,0:T(8,128)S(1)} copy-done((f32[64,16,256]{2,1,0:T(8,128)S(1)}, f32[64,16,256]{2,1,0:T(8,128)}, u32[]{:S(2)}) %copy-start) | copy-done | bytes 1048600
  2.0 0.0 copy-start.1
  2.0 1.2 %copy-done.1 = bf16[512,1024]{1,0:T(8,128)(2,1)S(1)} copy-done((bf16[512,1024]{1,0:T(8,128)(2,1)S(1)}, bf16[512,1024]{1,0:T(8,128)(2,1)}, u32[]{:S(2)}) %copy-start.1) | copy-done | bytes 1048600
  3.3 0.0 copy-start.2
  3.3 1.2 %copy-done.2 = bf16[512,1024]{1,0:T(8,128)(2,1)S(1)} copy-done((bf16[512,1024]{1,0:T(8,128)(2,1)S(1)}, bf16[512,1024]{1,0:T(8,128)(2,1)}, u32[]{:S(2)}) %copy-start.2) | copy-done | bytes 1048600
  4.5 0.0 copy-start.3
  4.5 0.9 %copy-done.3 = bf16[256,512]{1,0:T(8,128)(2,1)S(1)} copy-done((bf16[256,512]{1,0:T(8,128)(2,1)S(1)}, bf16[256,512]{1,0:T(8,128)(2,1)}, u32[]{:S(2)}) %copy-start.3) | copy-done | bytes 262168
  5.4 0.0 copy-start.4
  5.4 0.9 %copy-done.4 = bf16[256,512]{1,0:T(8,128)(2,1)S(1)} copy-done((bf16[256,512]{1,0:T(8,128)(2,1)S(1)}, bf16[256,512]{1,0:T(8,128)(2,1)}, u32[]{:S(2)}) %copy-start.4) | copy-done | bytes 262168
  6.4 0.0 copy-start.5
  6.4 0.9 %copy-done.5 = f32[256,128]{1,0:T(8,128)S(1)} copy-done((f32[256,128]{1,0:T(8,128)S(1)}, f32[256,128]{1,0:T(8,128)}, u32[]{:S(2)}) %copy-start.5) | copy-done | bytes 131096
  7.3 0.0 copy-start.6
  7.3 0.7 %copy-done.6 = s32[256]{0:T(256)S(1)} copy-done((s32[256]{0:T(256)S(1)}, s32[256]{0:T(256)}, u32[]{:S(2)}) %copy-start.6) | copy-done | bytes 1048
  8.0 50.1 %shard_map.100 = f32[256,128]{1,0:T(8,128)S(1)} custom-call(f32[256,128]{1,0:T(8,128)S(1)} %copy-done.5, s32[256,1]{1,0:T(8,128)S(1)} %copy.11.dest_ref, s32[1,256]{1,0:T(1,128)S(1)} %bitcast.1, f32[64,16,256]{2,1,0:T(8,128)S(1)} %copy-done, bf16[1024,2048]{1,0:T(8,128)(2,1)} %constant.12.clone.zh_hbm, bf16[1024,2048]{1,0:T(8,128)(2,1)} %constant.13.clone.zl_hbm, ...), custom_call_target="tpu_custom_call" | custom-call | tf_op jit(solution)/shard_map/pallas_call | solution.py:432
  58.1 0.7 %copy.13 = f32[256,128]{1,0:T(8,128)} copy(f32[256,128]{1,0:T(8,128)S(1)} %shard_map.100) | data formatting | bytes 262144
Async XLA Ops:
  0.8 1.2 %copy-start = (f32[64,16,256]{2,1,0:T(8,128)S(1)}, f32[64,16,256]{2,1,0:T(8,128)}, u32[]{:S(2)}) copy-start(f32[64,16,256]{2,1,0:T(8,128)} %green_hbm.1) | copy-start | bytes 3145732
  2.0 1.2 %copy-start.1 = (bf16[512,1024]{1,0:T(8,128)(2,1)S(1)}, bf16[512,1024]{1,0:T(8,128)(2,1)}, u32[]{:S(2)}) copy-start(bf16[512,1024]{1,0:T(8,128)(2,1)} %constant.15.clone.yl_hbm) | copy-start | bytes 3145732
  3.3 1.2 %copy-start.2 = (bf16[512,1024]{1,0:T(8,128)(2,1)S(1)}, bf16[512,1024]{1,0:T(8,128)(2,1)}, u32[]{:S(2)}) copy-start(bf16[512,1024]{1,0:T(8,128)(2,1)} %constant.14.clone.yh_hbm) | copy-start | bytes 3145732
  4.5 0.9 %copy-start.3 = (bf16[256,512]{1,0:T(8,128)(2,1)S(1)}, bf16[256,512]{1,0:T(8,128)(2,1)}, u32[]{:S(2)}) copy-start(bf16[256,512]{1,0:T(8,128)(2,1)} %constant.17.clone.xl_hbm) | copy-start | bytes 786436
  5.4 0.9 %copy-start.4 = (bf16[256,512]{1,0:T(8,128)(2,1)S(1)}, bf16[256,512]{1,0:T(8,128)(2,1)}, u32[]{:S(2)}) copy-start(bf16[256,512]{1,0:T(8,128)(2,1)} %constant.16.clone.xh_hbm) | copy-start | bytes 786436
  6.4 0.9 %copy-start.5 = (f32[256,128]{1,0:T(8,128)S(1)}, f32[256,128]{1,0:T(8,128)}, u32[]{:S(2)}) copy-start(f32[256,128]{1,0:T(8,128)} %charge_ref.1) | copy-start | bytes 393220
  7.3 0.7 %copy-start.6 = (s32[256]{0:T(256)S(1)}, s32[256]{0:T(256)}, u32[]{:S(2)}) copy-start(s32[256]{0:T(256)} %param.12) | copy-start | bytes 3076

commit v3 on v2

--- a/solution.py
+++ b/solution.py
@@ -209,6 +209,9 @@
     slots = charge_ref.shape[0]
     cap = charge_send.shape[1]
     rows = n_dev * cap
+    side = n_dev // 2
+    near = me // side
+    far = 1 - near
     blocks = CXP * CYP * NZP // LANES
 
     barrier = pltpu.get_barrier_semaphore()
@@ -232,41 +235,62 @@
     for load in loads:
         load.start()
 
-    def block_copy(send, recv, number, peer):
+    def block_copy(send, recv, number, peer, part):
         return pltpu.make_async_remote_copy(
             src_ref=send.at[peer],
             dst_ref=recv.at[me],
             send_sem=send_sems.at[number],
-            recv_sem=recv_sems.at[number],
+            recv_sem=recv_sems.at[number, part],
             device_id=(peer // n_pz, lax.rem(peer, n_pz)),
             device_id_type=MESH,
         )
 
+    def send_far(send, recv, number):
+        def body(step, carry):
+            block_copy(send, recv, number, far * side + lax.rem(me + step, side), 1).start()
+            return carry
+
+        lax.fori_loop(0, side, body, 0)
+
+    def send_near(send, recv, number):
+        def body(step, carry):
+            block_copy(send, recv, number, near * side + lax.rem(me + step, side), 0).start()
+            return carry
+
+        lax.fori_loop(1, side, body, 0)
+        recv[me] = send[me]
+
     def send_all(send, recv, number):
-        def body(step, carry):
-            block_copy(send, recv, number, lax.rem(me + step, n_dev)).start()
-            return carry
-
-        lax.fori_loop(1, n_dev, body, 0)
-        recv[me] = send[me]
-
-    def all_of(send, recv, number, count):
+        send_far(send, recv, number)
+        send_near(send, recv, number)
+
+    def all_of(send, recv, number, count, part=0):
         return pltpu.make_async_remote_copy(
             src_ref=send.at[pl.ds(0, count)],
             dst_ref=recv.at[pl.ds(0, count)],
             send_sem=send_sems.at[number],
-            recv_sem=recv_sems.at[number],
+            recv_sem=recv_sems.at[number, part],
             device_id=(mi, mj),
             device_id_type=MESH,
         )
 
-    dest = dest_ref[...]
-    named = one(dest == iota((slots, LANES), 1))
+    def wait_near(send, recv, number):
+        all_of(send, recv, number, side - 1, 0).wait_recv()
+
+    def wait_far(send, recv, number):
+        all_of(send, recv, number, side, 1).wait_recv()
+
+    def wait_both(send, recv, number):
+        wait_near(send, recv, number)
+        wait_far(send, recv, number)
+
+    dest_row = dest_ref[...].astype(jnp.float32)
+    dest = as_column(dest_row)
+    named = one(dest == iota((slots, LANES), 1).astype(jnp.float32))
     before = one(iota((slots, slots), 1) < iota((slots, slots), 0))
     rank = jnp.sum(mm(before, named) * named.astype(jnp.float32), axis=1, keepdims=True)
-    place = dest.astype(jnp.float32) * cap + rank
+    place = dest * cap + rank
     ids = ids_ref[...].astype(jnp.float32) + 1.0
-    dest_row = as_row(dest.astype(jnp.float32))
     owned = jnp.where(dest_row == iota((n_dev, slots), 0).astype(jnp.float32), ids, 0.0)
     ranked = one(rank == iota((slots, LANES), 1).astype(jnp.float32))
     ids_send[...] = mm(owned.astype(jnp.bfloat16), ranked).reshape(n_dev, 1, LANES)
@@ -289,16 +313,18 @@
             src_ref=green_send.at[target],
             dst_ref=green_recv.at[mi],
             send_sem=send_sems.at[2],
-            recv_sem=recv_sems.at[2],
+            recv_sem=recv_sems.at[2, 0],
             device_id=(target, mj),
             device_id_type=MESH,
         )
 
-    for step in range(1, n_px):
-        green_copy(lax.rem(mi + step, n_px)).start()
+    pair_start = near * 2
+    for step in range(2):
+        green_copy(far * 2 + step).start()
+    green_copy(pair_start + 1 - lax.rem(mi, 2)).start()
     green_recv[mi] = green_send[mi]
 
-    all_of(ids_send, ids_recv, 0, n_dev - 1).wait_recv()
+    wait_both(ids_send, ids_recv, 0)
     line = iota((rows, n_dev), 0)
     spread = mm(one(line // cap == iota((rows, n_dev), 1)), ids_recv[...].reshape(n_dev, LANES).astype(jnp.bfloat16))
     own_lane = iota((rows, LANES), 1) == lax.rem(iota((rows, LANES), 0), cap)
@@ -310,7 +336,7 @@
 
     taking = one(ids == target_of(iota((rows, blocks), 1)))
     placing = one(as_row(ids) == target_of(iota((blocks, rows), 0)))
-    all_of(charge_send, charge_recv, 1, n_dev - 1).wait_recv()
+    wait_both(charge_send, charge_recv, 1)
     field = mm_pick(placing, charge_recv[...].reshape(rows, LANES))
     field = jnp.concatenate([field[lines * c : lines * (c + 1)] for c in range(NZP // LANES)], axis=1)
 
@@ -320,27 +346,35 @@
     loads[2].wait()
     first = iota((lines // 2, LANES), 1) < GROUP
 
-    def forward(step, carry):
-        j = lax.rem(mj + step, n_pz)
-        columns = pl.ds(pl.multiple_of(j * 256, 256), 256)
-        both = mm(f_both, zh[:, columns])
-        total = both[:lines] + (both[lines:] + mm(f_high, zl[:, columns]))
-        for pair in range(2):
-            tile = total[:, pair * LANES : (pair + 1) * LANES]
-            low, high = tile[: lines // 2], tile[lines // 2 :]
-            low_turned, high_turned = pltpu.roll(low, GROUP, 1), pltpu.roll(high, GROUP, 1)
-            spec_send[2 * pair * n_pz + j] = jnp.where(first, low, high_turned)
-            spec_send[(2 * pair + 1) * n_pz + j] = jnp.where(first, low_turned, high)
-        for turn in range(n_px):
-            peer = lax.rem(mi + turn, n_px) * n_pz + j
-
-            @pl.when(peer != me)
-            def _():
-                block_copy(spec_send, spec_recv, 3, peer).start()
-
-        return carry
-
-    lax.fori_loop(0, n_pz, forward, 0)
+    def forward(half, part):
+        def body(step, carry):
+            two = lax.rem(mj // 2 + step, n_pz // 2)
+            columns = pl.ds(pl.multiple_of(half * NZP + two * 256, 256), 256)
+            both = mm(f_both, zh[:, columns])
+            total = both[:lines] + (both[lines:] + mm(f_high, zl[:, columns]))
+            for t in range(2):
+                j = two * 2 + t
+                tile = total[:, t * LANES : (t + 1) * LANES]
+                low, high = tile[: lines // 2], tile[lines // 2 :]
+                low_turned, high_turned = pltpu.roll(low, GROUP, 1), pltpu.roll(high, GROUP, 1)
+                at = half * side + j
+                spec_send[at] = jnp.where(first, low, high_turned)
+                spec_send[at + n_pz] = jnp.where(first, low_turned, high)
+                for peer in (at, at + n_pz):
+                    if part == 1:
+                        block_copy(spec_send, spec_recv, 3, peer, 1).start()
+                    else:
+
+                        @pl.when(peer != me)
+                        def _():
+                            block_copy(spec_send, spec_recv, 3, peer, 0).start()
+
+            return carry
+
+        lax.fori_loop(0, n_pz // 2, body, 0)
+
+    forward(far, 1)
+    forward(near, 0)
     spec_recv[me] = spec_send[me]
 
     all_of(green_send, green_recv, 2, n_px - 1).wait_recv()
@@ -362,9 +396,16 @@
 
     for load in loads[3:]:
         load.wait()
-    all_of(spec_send, spec_recv, 3, n_dev - 1).wait_recv()
-    planes = jnp.transpose(spec_recv[...].reshape(n_dev * 16, LANES))
-    planes = mm_left(planes, yh[...], yl[...])
+
+    def side_planes(half):
+        taken = spec_recv[pl.ds(half * side, side)].reshape(side * 16, LANES)
+        table_rows = pl.ds(pl.multiple_of(half * (side * 16), side * 16), side * 16)
+        return mm_left(jnp.transpose(taken), yh[table_rows, :], yl[table_rows, :])
+
+    wait_near(spec_send, spec_recv, 3)
+    planes = side_planes(near)
+    wait_far(spec_send, spec_recv, 3)
+    planes = planes + side_planes(far)
     groups = 2 * n_px
     planes = jnp.concatenate(
         [
@@ -388,24 +429,37 @@
     )
     p_high, p_low = halves(planes)
     right = ((1,), (1,))
-    planes = mm(yh[...], p_high, right) + (mm(yh[...], p_low, right) + mm(yl[...], p_high, right))
-    back_send[...] = planes.reshape(n_dev, 16, LANES)
-    send_all(back_send, back_recv, 4)
-
-    all_of(back_send, back_recv, 4, n_dev - 1).wait_recv()
-    pieces = []
-    for j in range(n_pz):
-        for pair in range(2):
-            left, other = back_recv[2 * pair * n_pz + j], back_recv[(2 * pair + 1) * n_pz + j]
+
+    def side_back(half):
+        table_rows = pl.ds(pl.multiple_of(half * (side * 16), side * 16), side * 16)
+        high, low = yh[table_rows, :], yl[table_rows, :]
+        given = mm(high, p_high, right) + (mm(high, p_low, right) + mm(low, p_high, right))
+        back_send[pl.ds(half * side, side)] = given.reshape(side, 16, LANES)
+
+    side_back(far)
+    send_far(back_send, back_recv, 4)
+    side_back(near)
+    send_near(back_send, back_recv, 4)
+
+    def side_phi(half):
+        pieces = []
+        for j in range(n_pz):
+            left, other = back_recv[half * side + j], back_recv[half * side + n_pz + j]
             low = jnp.where(first, left, pltpu.roll(other, GROUP, 1))
             high = jnp.where(first, pltpu.roll(left, GROUP, 1), other)
             pieces.append(jnp.concatenate((low, high), axis=0))
-    phi = mm_left(jnp.concatenate(pieces, axis=1), zh[...], zl[...], right)
+        columns = pl.ds(pl.multiple_of(half * NZP, NZP), NZP)
+        return mm_left(jnp.concatenate(pieces, axis=1), zh[:, columns], zl[:, columns], right)
+
+    wait_near(back_send, back_recv, 4)
+    phi = side_phi(near)
+    wait_far(back_send, back_recv, 4)
+    phi = phi + side_phi(far)
     phi = jnp.concatenate([phi[:, c * LANES : (c + 1) * LANES] for c in range(NZP // LANES)], axis=0)
     out_send[...] = mm_pick(taking, phi).reshape(n_dev, cap, LANES)
     send_all(out_send, out_recv, 5)
     unpacking = one(place == iota((slots, rows), 1).astype(jnp.float32))
-    all_of(out_send, out_recv, 5, n_dev - 1).wait_recv()
+    wait_both(out_send, out_recv, 5)
     out_ref[...] = mm_pick(unpacking, out_recv[...].reshape(rows, LANES))
 
     all_of(ids_send, ids_recv, 0, n_dev - 1).wait_send()
@@ -422,13 +476,15 @@
     slots = charge.shape[0]
     cap = 2 * slots // n_dev
     y_table, x_table = plane_tables(n_px, n_pz)
+    z_table = long_table().reshape(NZP, n_pz, 2, 2 * GROUP).transpose(0, 2, 1, 3)
+    z_table = z_table.reshape(NZP, 2 * NZP) / math.sqrt(2 * NZP)
     tables = [
         piece
-        for table in (long_table() / math.sqrt(2 * NZP), y_table, x_table)
+        for table in (z_table, y_table, x_table)
         for piece in split_table(table)
     ]
     exchange = lambda lead, rows: [pltpu.VMEM((lead, rows, LANES), jnp.float32)] * 2
-    vmem, anywhere = pl.BlockSpec(memory_space=pltpu.VMEM), pl.BlockSpec(memory_space=pl.ANY)
+    vmem, anywhere = pl.BlockSpec(memory_space=pltpu.VMEM), pl.BlockSpec(memory_space=pltpu.HBM)
     return pl.pallas_call(
         functools.partial(fused, n_px, n_pz),
         out_shape=jax.ShapeDtypeStruct(charge.shape, jnp.float32),
@@ -446,12 +502,12 @@
             pltpu.VMEM((2 * n_px * GROUP, 2 * HALF * KEPT), jnp.float32),
             pltpu.SemaphoreType.DMA((7,)),
             pltpu.SemaphoreType.DMA((6,)),
-            pltpu.SemaphoreType.DMA((6,)),
+            pltpu.SemaphoreType.DMA((6, 2)),
         ],
         compiler_params=pltpu.CompilerParams(
             collective_id=0, has_side_effects=True, vmem_limit_bytes=48 * 1024 * 1024
         ),
-    )(charge, dest, local_ids.reshape(1, slots), green_hat, *tables)
+    )(charge, dest.reshape(1, slots), local_ids.reshape(1, slots), green_hat, *tables)
 
 
 def solution(mesh):

time: 59.6 us -> 60.7 us (1.018)
  Pallas kernels: 50.1 us -> 51.9 us
    pallas_call x1, Pallas kernels: 50.1 us -> 51.9 us  [local_fused(): pl.pallas_call(functools.partial(fused, n_px, n_pz), out_shape=jax.ShapeD...]
    unnamed x16 -> x17, local copies, waits for them, and re-layouts: 8.61 us -> 8.49 us
where the time goes in v3:
time: 60.7 us; the launch traced here: 60.4 us
  Pallas kernels  51.9 us (86%)
  local copies, waits for them, and re-layouts  8.49 us (14%)
    pallas_call x1, Pallas kernels, local_fused(): pl.pallas_call(functools.partial(fused, n_px, n_pz), out_shape=jax.ShapeD...  51.9 us
    unnamed x17, local copies, waits for them, and re-layouts  8.49 us

profile of v3, /device:TPU:0, one launch (start us, length us, event | category | flops | bytes accessed | tf_op | source)
XLA Modules:
  0.0 60.4 jit_solution(6550197358555713603)
XLA Ops:
  0.0 0.0 copy-start
  0.0 1.2 %copy-done = f32[64,16,256]{2,1,0:T(8,128)S(1)} copy-done((f32[64,16,256]{2,1,0:T(8,128)S(1)}, f32[64,16,256]{2,1,0:T(8,128)}, u32[]{:S(2)}) %copy-start) | copy-done | bytes 1048600
  1.2 0.0 copy-start.1
  1.2 1.2 %copy-done.1 = bf16[512,1024]{1,0:T(8,128)(2,1)S(1)} copy-done((bf16[512,1024]{1,0:T(8,128)(2,1)S(1)}, bf16[512,1024]{1,0:T(8,128)(2,1)}, u32[]{:S(2)}) %copy-start.1) | copy-done | bytes 1048600
  2.5 0.0 copy-start.2
  2.5 1.2 %copy-done.2 = bf16[512,1024]{1,0:T(8,128)(2,1)S(1)} copy-done((bf16[512,1024]{1,0:T(8,128)(2,1)S(1)}, bf16[512,1024]{1,0:T(8,128)(2,1)}, u32[]{:S(2)}) %copy-start.2) | copy-done | bytes 1048600
  3.7 0.0 copy-start.3
  3.7 0.9 %copy-done.3 = bf16[256,512]{1,0:T(8,128)(2,1)S(1)} copy-done((bf16[256,512]{1,0:T(8,128)(2,1)S(1)}, bf16[256,512]{1,0:T(8,128)(2,1)}, u32[]{:S(2)}) %copy-start.3) | copy-done | bytes 262168
  4.6 0.0 copy-start.4
  4.6 0.9 %copy-done.4 = bf16[256,512]{1,0:T(8,128)(2,1)S(1)} copy-done((bf16[256,512]{1,0:T(8,128)(2,1)S(1)}, bf16[256,512]{1,0:T(8,128)(2,1)}, u32[]{:S(2)}) %copy-start.4) | copy-done | bytes 262168
  5.6 0.0 copy-start.5
  5.6 0.9 %copy-done.5 = f32[256,128]{1,0:T(8,128)S(1)} copy-done((f32[256,128]{1,0:T(8,128)S(1)}, f32[256,128]{1,0:T(8,128)}, u32[]{:S(2)}) %copy-start.5) | copy-done | bytes 131096
  6.5 0.0 copy-start.6
  6.5 0.7 %copy-done.6 = s32[256,1]{0,1:T(1,128)S(1)} copy-done((s32[256,1]{0,1:T(1,128)S(1)}, s32[256,1]{0,1:T(1,128)}, u32[]{:S(2)}) %copy-start.6) | copy-done | bytes 1048
  7.2 0.0 copy-start.7
  7.2 0.7 %copy-done.7 = s32[256]{0:T(256)S(1)} copy-done((s32[256]{0:T(256)S(1)}, s32[256]{0:T(256)}, u32[]{:S(2)}) %copy-start.7) | copy-done | bytes 1048
  7.8 51.9 %shard_map.100 = f32[256,128]{1,0:T(8,128)S(1)} custom-call(f32[256,128]{1,0:T(8,128)S(1)} %copy-done.5, s32[1,256]{1,0:T(1,128)S(1)} %bitcast.2, s32[1,256]{1,0:T(1,128)S(1)} %bitcast.3, f32[64,16,256]{2,1,0:T(8,128)S(1)} %copy-done, bf16[1024,2048]{1,0:T(8,128)(2,1)} %constant.12.clone.zh_hbm, bf16[1024,2048]{1,0:T(8,128)(2,1)} %constant.13.clone.zl_hbm, ...), custom_call_target="tpu_custom_call" | custom-call | tf_op jit(solution)/shard_map/pallas_call | solution.py:488
  59.7 0.7 %copy.12 = f32[256,128]{1,0:T(8,128)} copy(f32[256,128]{1,0:T(8,128)S(1)} %shard_map.100) | data formatting | bytes 262144
Async XLA Ops:
  0.0 1.2 %copy-start = (f32[64,16,256]{2,1,0:T(8,128)S(1)}, f32[64,16,256]{2,1,0:T(8,128)}, u32[]{:S(2)}) copy-start(f32[64,16,256]{2,1,0:T(8,128)} %green_hbm.1) | copy-start | bytes 3145732
  1.2 1.2 %copy-start.1 = (bf16[512,1024]{1,0:T(8,128)(2,1)S(1)}, bf16[512,1024]{1,0:T(8,128)(2,1)}, u32[]{:S(2)}) copy-start(bf16[512,1024]{1,0:T(8,128)(2,1)} %constant.15.clone.yl_hbm) | copy-start | bytes 3145732
  2.5 1.2 %copy-start.2 = (bf16[512,1024]{1,0:T(8,128)(2,1)S(1)}, bf16[512,1024]{1,0:T(8,128)(2,1)}, u32[]{:S(2)}) copy-start(bf16[512,1024]{1,0:T(8,128)(2,1)} %constant.14.clone.yh_hbm) | copy-start | bytes 3145732
  3.7 0.9 %copy-start.3 = (bf16[256,512]{1,0:T(8,128)(2,1)S(1)}, bf16[256,512]{1,0:T(8,128)(2,1)}, u32[]{:S(2)}) copy-start(bf16[256,512]{1,0:T(8,128)(2,1)} %constant.17.clone.xl_hbm) | copy-start | bytes 786436
  4.6 0.9 %copy-start.4 = (bf16[256,512]{1,0:T(8,128)(2,1)S(1)}, bf16[256,512]{1,0:T(8,128)(2,1)}, u32[]{:S(2)}) copy-start(bf16[256,512]{1,0:T(8,128)(2,1)} %constant.16.clone.xh_hbm) | copy-start | bytes 786436
  5.6 0.9 %copy-start.5 = (f32[256,128]{1,0:T(8,128)S(1)}, f32[256,128]{1,0:T(8,128)}, u32[]{:S(2)}) copy-start(f32[256,128]{1,0:T(8,128)} %charge_ref.1) | copy-start | bytes 393220
  6.5 0.7 %copy-start.6 = (s32[256,1]{0,1:T(1,128)S(1)}, s32[256,1]{0,1:T(1,128)}, u32[]{:S(2)}) copy-start(s32[256,1]{0,1:T(1,128)} %param.11) | copy-start | bytes 3076
  7.2 0.7 %copy-start.7 = (s32[256]{0:T(256)S(1)}, s32[256]{0:T(256)}, u32[]{:S(2)}) copy-start(s32[256]{0:T(256)} %param.12) | copy-start | bytes 3076

commit v4 on v3

--- a/solution.py
+++ b/solution.py
@@ -142,15 +142,17 @@
 
 
 def plane_tables(n_px, n_pz):
-    starts = np.array([0, 16, 33, 49])
-    raw = (starts[:, None] + np.arange(KEPT)[None, :]).reshape(-1)
-    folded = np.minimum(raw, 2 * WIDE - raw)
-    frequencies = np.concatenate((folded, np.where(folded == 0, WIDE, folded)))
-    sine = np.concatenate((np.zeros(HALF, bool), folded != 0))
-    rows = unit_rows(frequencies, sine, WIDE).reshape(2 * n_px, KEPT, n_pz, CYP)
-    eye_i, eye_a = np.eye(n_px), np.eye(4)
-    y_table = np.einsum("gqjb,iI,aA->ijabgIqA", rows, eye_i, eye_a)
-    y_table = y_table.reshape(n_px * n_pz * 16, 2 * n_px * n_px * KEPT * 4)
+    y_tables = []
+    for half in range(2):
+        raw = half * WIDE + np.arange(HALF)
+        folded = np.minimum(raw, 2 * WIDE - raw)
+        lone = folded == folded[0]
+        frequencies = np.concatenate((folded, np.where(lone, WIDE - folded[0], folded)))
+        sine = np.concatenate((np.zeros(HALF, bool), ~lone))
+        rows = unit_rows(frequencies, sine, WIDE).reshape(2 * n_px, KEPT, n_pz, CYP)
+        table = np.einsum("gqjb,iI,aA->ijabgIqA", rows, np.eye(n_px), np.eye(4))
+        y_tables.append(table.reshape(n_px * n_pz * 16, 2 * n_px * n_px * KEPT * 4))
+    y_table = np.stack(y_tables)
     base = np.arange(HALF)
     frequencies = np.concatenate((base, np.where(base == 0, WIDE, base)))
     sine = np.concatenate((np.zeros(HALF, bool), base != 0))
@@ -200,8 +202,8 @@
 def fused(
     n_px, n_pz, charge_ref, dest_ref, ids_ref, green_hbm, zh_hbm, zl_hbm, yh_hbm, yl_hbm, xh_hbm,
     xl_hbm, out_ref, green, zh, zl, yh, yl, xh, xl, ids_send, ids_recv, charge_send, charge_recv,
-    green_send, green_recv, spec_send, spec_recv, back_send, back_recv, out_send, out_recv, scale,
-    load_sems, send_sems, recv_sems
+    green_send, green_recv, edge_recv, spec_send, spec_recv, back_send, back_recv, out_send, out_recv, scale,
+    load_sems, green_sems, send_sems, recv_sems
 ):
     n_dev = n_px * n_pz
     mi, mj = lax.axis_index("px"), lax.axis_index("pz")
@@ -228,8 +230,8 @@
     loads = [
         pltpu.make_async_copy(source, target, load_sems.at[number])
         for number, (source, target) in enumerate((
-            (green_hbm.at[pl.ds(0, 40)], green), (zh_hbm, zh), (zl_hbm, zl), (yh_hbm, yh),
-            (yl_hbm, yl), (xh_hbm, xh), (xl_hbm, xl),
+            (green_hbm.at[pl.ds(0, 40)], green), (zh_hbm, zh), (zl_hbm, zl), (yh_hbm.at[near], yh),
+            (yl_hbm.at[near], yl), (xh_hbm, xh), (xl_hbm, xl),
         ))
     ]
     for load in loads:
@@ -301,28 +303,38 @@
     send_all(charge_send, charge_recv, 1)
 
     loads[0].wait()
-    shifted = mi >= n_px // 2
-    kept = jnp.where(shifted, green[0:33, 1:9, :], green[0:33, 0:8, :])
-    wide = jnp.transpose(kept[0:HALF].reshape(HALF * KEPT, 256))
-    edge = green[0:40, 0, :]
-    edge = jnp.concatenate((kept[HALF], edge, jnp.zeros((LANES - 48, 256), jnp.float32)), axis=0)
-    green_send[...] = jnp.concatenate((wide, jnp.transpose(edge)), axis=1).reshape(n_px, GROUP, 384)
-
-    def green_copy(target):
+    wide = [jnp.transpose(green[0:HALF, t * KEPT : (t + 1) * KEPT, :].reshape(HALF * KEPT, 256)) for t in range(2)]
+    edge = jnp.concatenate((green[HALF], green[0:40, 0, :], jnp.zeros((LANES - 56, 256), jnp.float32)), axis=0)
+    green_send[...] = jnp.concatenate((*wide, jnp.transpose(edge)), axis=1).reshape(n_px, GROUP, 640)
+    odd = lax.rem(mi, 2)
+    partner = mi + 1 - 2 * odd
+    green_copy = pltpu.make_async_remote_copy(
+        src_ref=green_send.at[partner],
+        dst_ref=green_recv.at[odd],
+        send_sem=green_sems.at[0],
+        recv_sem=green_sems.at[3],
+        device_id=(partner, mj),
+        device_id_type=MESH,
+    )
+    green_copy.start()
+
+    def edge_copy(step):
+        target = far * 2 + step
         return pltpu.make_async_remote_copy(
-            src_ref=green_send.at[target],
-            dst_ref=green_recv.at[mi],
-            send_sem=send_sems.at[2],
-            recv_sem=recv_sems.at[2, 0],
+            src_ref=green_send.at[target, :, pl.ds(512, LANES)],
+            dst_ref=edge_recv,
+            send_sem=green_sems.at[1 + step],
+            recv_sem=green_sems.at[4],
             device_id=(target, mj),
             device_id_type=MESH,
         )
 
-    pair_start = near * 2
-    for step in range(2):
-        green_copy(far * 2 + step).start()
-    green_copy(pair_start + 1 - lax.rem(mi, 2)).start()
-    green_recv[mi] = green_send[mi]
+    @pl.when(odd == 0)
+    def _():
+        for step in range(2):
+            edge_copy(step).start()
+
+    green_recv[odd] = green_send[mi]
 
     wait_both(ids_send, ids_recv, 0)
     line = iota((rows, n_dev), 0)
@@ -377,22 +389,27 @@
     forward(near, 0)
     spec_recv[me] = spec_send[me]
 
-    all_of(green_send, green_recv, 2, n_px - 1).wait_recv()
-    lane = iota((GROUP, 256), 1)
+    green_copy.wait_recv()
+    edge_copy(0).wait_recv()
     source, target = iota((LANES, 512), 0), iota((LANES, 512), 1)
-    wanted = jnp.where(target == 256, HALF, lax.rem(target, 256) // KEPT) + KEPT
+    wanted = jnp.where(target == 256, HALF, lax.rem(target, 256) // KEPT) + 2 * KEPT
     picking = one((source == wanted) & (lax.rem(target, KEPT) == 0))
-    e_high, e_low = halves(green_recv[2, :, 256:384])
-    e_rest = (green_recv[2, :, 256:384] - e_high.astype(jnp.float32) - e_low.astype(jnp.float32)).astype(jnp.bfloat16)
-    nyquist = mm(e_high, picking) + (mm(e_low, picking) + mm(e_rest, picking))
-    for i in range(n_px):
-        wide = green_recv[i, :, 0:256]
-        edge = jnp.concatenate((green_recv[i, :, 256:384], wide[:, LANES:]), axis=1)
-        full = jnp.concatenate((wide, jnp.where(lane < KEPT, edge, wide)), axis=1)
-        scale[i * GROUP : (i + 1) * GROUP, :] = full
-        if i == 0:
-            full = jnp.where(lax.rem(iota((GROUP, 512), 1), KEPT) == 0, nyquist, full)
-        scale[(n_px + i) * GROUP : (n_px + i + 1) * GROUP, :] = full
+    e_high, e_low = halves(edge_recv[...])
+    lone = mm(e_high, picking) + mm(e_low, picking)
+    lane = iota((GROUP, LANES), 1)
+    for parity in range(2):
+        edge = green_recv[parity, :, 512:640]
+        for t in range(2):
+            wide = green_recv[parity, :, t * 256 : (t + 1) * 256]
+            turned = edge if t == 0 else pltpu.roll(edge, LANES - KEPT, 1)
+            start = jnp.where(lane < KEPT, turned, wide[:, :LANES])
+            full = jnp.concatenate((wide, start, wide[:, LANES:]), axis=1)
+            at = (2 * parity + t) * GROUP
+            scale[at : at + GROUP, :] = full
+            if parity == 0 and t == 0:
+                full = jnp.where(lax.rem(iota((GROUP, 512), 1), KEPT) == 0, lone, full)
+            at = at + n_px * GROUP
+            scale[at : at + GROUP, :] = full
 
     for load in loads[3:]:
         load.wait()
@@ -464,7 +481,13 @@
 
     all_of(ids_send, ids_recv, 0, n_dev - 1).wait_send()
     all_of(charge_send, charge_recv, 1, n_dev - 1).wait_send()
-    all_of(green_send, green_recv, 2, n_px - 1).wait_send()
+    green_copy.wait_send()
+
+    @pl.when(odd == 0)
+    def _():
+        for step in range(2):
+            edge_copy(step).wait_send()
+
     all_of(spec_send, spec_recv, 3, n_dev - 1).wait_send()
     all_of(back_send, back_recv, 4, n_dev - 1).wait_send()
     all_of(out_send, out_recv, 5, n_dev - 1).wait_send()
@@ -492,20 +515,23 @@
         out_specs=vmem,
         scratch_shapes=[
             pltpu.VMEM((40,) + green_hat.shape[1:], jnp.float32),
-            *[pltpu.VMEM(table.shape, jnp.bfloat16) for table in tables],
+            *[pltpu.VMEM(table.shape[-2:], jnp.bfloat16) for table in tables],
             *exchange(n_dev, 1),
             *exchange(n_dev, cap),
-            *[pltpu.VMEM((n_px, GROUP, 384), jnp.float32)] * 2,
+            pltpu.VMEM((n_px, GROUP, 640), jnp.float32),
+            pltpu.VMEM((2, GROUP, 640), jnp.float32),
+            pltpu.VMEM((GROUP, LANES), jnp.float32),
             *exchange(n_dev, 16),
             *exchange(n_dev, 16),
             *exchange(n_dev, cap),
             pltpu.VMEM((2 * n_px * GROUP, 2 * HALF * KEPT), jnp.float32),
             pltpu.SemaphoreType.DMA((7,)),
+            pltpu.SemaphoreType.DMA((5,)),
             pltpu.SemaphoreType.DMA((6,)),
             pltpu.SemaphoreType.DMA((6, 2)),
         ],
         compiler_params=pltpu.CompilerParams(
-            collective_id=0, has_side_effects=True, vmem_limit_bytes=48 * 1024 * 1024
+            collective_id=0, has_side_effects=True, vmem_limit_bytes=64 * 1024 * 1024
         ),
     )(charge, dest.reshape(1, slots), local_ids.reshape(1, slots), green_hat, *tables)
 

time: 60.7 us -> 50.7 us (0.84)
  local copies, waits for them, and re-layouts: 8.49 us -> 1.57 us
  Pallas kernels: 51.9 us -> 49 us
    unnamed x17 -> x1, local copies, waits for them, and re-layouts: 8.49 us -> 1.57 us
    pallas_call x1, Pallas kernels: 51.9 us -> 49 us  [local_fused(): pl.pallas_call(functools.partial(fused, n_px, n_pz), out_shape=jax.ShapeD...]
where the time goes in v4:
time: 50.7 us; the launch traced here: 50.6 us
  Pallas kernels  49 us (97%)
  local copies, waits for them, and re-layouts  1.57 us (3%)
    pallas_call x1, Pallas kernels, local_fused(): pl.pallas_call(functools.partial(fused, n_px, n_pz), out_shape=jax.ShapeD...  49 us
    unnamed x1, local copies, waits for them, and re-layouts  1.57 us

profile of v4, /device:TPU:0, one launch (start us, length us, event | category | flops | bytes accessed | tf_op | source)
XLA Modules:
  0.0 50.6 jit_solution(6458634516436336181)
XLA Ops:
  0.0 49.0 %shard_map.100 = f32[256,128]{1,0:T(8,128)} custom-call(f32[256,128]{1,0:T(8,128)} %charge_ref.1, s32[1,256]{1,0:T(1,128)} %bitcast.2, s32[1,256]{1,0:T(1,128)} %bitcast.3, f32[64,16,256]{2,1,0:T(8,128)} %green_hbm.1, bf16[1024,2048]{1,0:T(8,128)(2,1)} %constant.12.clone.zh_hbm, bf16[1024,2048]{1,0:T(8,128)(2,1)} %constant.13.clone.zl_hbm, ...), custom_call_target="tpu_custom_call" | custom-call | tf_op jit(solution)/shard_map/pallas_call | solution.py:511
  49.0 1.6 %copy.12 = f32[256,128]{1,0:T(8,128)} copy(f32[256,128]{1,0:T(8,128)} %shard_map.100) | data formatting | bytes 262144

commit v5 on v4

--- a/solution.py
+++ b/solution.py
@@ -139,6 +139,15 @@
     angle = (frequencies[:, None] * np.arange(wide)[None, :] % period) * (2.0 * math.pi / period)
     weight = np.where((frequencies == 0) | (frequencies == wide), 1.0, 2.0) / period
     return np.where(is_sine[:, None], np.sin(angle), np.cos(angle)) * np.sqrt(weight)[:, None]
+
+
+def folded_table():
+    k = np.arange(2 * NZP)[None, :]
+    frequency = np.minimum(k, 2 * NZP - k)
+    odd = 2 * np.arange(NZP // 2)[:, None] - (NZP - 1)
+    angle = (frequency * odd % (4 * NZP)) * (2.0 * math.pi / (4 * NZP))
+    weight = np.where((frequency == 0) | (frequency == NZP), 1.0, 2.0) / (2 * NZP)
+    return np.where(k < NZP, np.cos(angle), np.sin(angle)) * np.sqrt(weight)
 
 
 def plane_tables(n_px, n_pz):
@@ -202,7 +211,7 @@
 def fused(
     n_px, n_pz, charge_ref, dest_ref, ids_ref, green_hbm, zh_hbm, zl_hbm, yh_hbm, yl_hbm, xh_hbm,
     xl_hbm, out_ref, green, zh, zl, yh, yl, xh, xl, ids_send, ids_recv, charge_send, charge_recv,
-    green_send, green_recv, edge_recv, spec_send, spec_recv, back_send, back_recv, out_send, out_recv, scale,
+    green_send, green_recv, edge_recv, spec_send, spec_recv, back_send, back_recv, out_send, out_recv, scale, folded,
     load_sems, green_sems, send_sems, recv_sems
 ):
     n_dev = n_px * n_pz
@@ -350,10 +359,19 @@
     placing = one(as_row(ids) == target_of(iota((blocks, rows), 0)))
     wait_both(charge_send, charge_recv, 1)
     field = mm_pick(placing, charge_recv[...].reshape(rows, LANES))
-    field = jnp.concatenate([field[lines * c : lines * (c + 1)] for c in range(NZP // LANES)], axis=1)
-
-    f_high, f_low = halves(field)
-    f_both = jnp.concatenate((f_high, f_low), axis=0)
+    mirror = one(iota((LANES, LANES), 0) + iota((LANES, LANES), 1) == LANES - 1)
+    pieces_z = NZP // LANES
+    middle = lines * pieces_z // 2
+    front = field[:middle]
+    m_high, m_low = halves(field[middle:])
+    rear = mm(m_high, mirror) + mm(m_low, mirror)
+    front = jnp.concatenate([front[lines * c : lines * (c + 1)] for c in range(pieces_z // 2)], axis=1)
+    rear = jnp.concatenate(
+        [rear[lines * c : lines * (c + 1)] for c in range(pieces_z // 2 - 1, -1, -1)], axis=1
+    )
+
+    for odd_part, part in enumerate((front + rear, front - rear)):
+        folded[odd_part] = jnp.concatenate(halves(part), axis=0)
     loads[1].wait()
     loads[2].wait()
     first = iota((lines // 2, LANES), 1) < GROUP
@@ -362,8 +380,9 @@
         def body(step, carry):
             two = lax.rem(mj // 2 + step, n_pz // 2)
             columns = pl.ds(pl.multiple_of(half * NZP + two * 256, 256), 256)
-            both = mm(f_both, zh[:, columns])
-            total = both[:lines] + (both[lines:] + mm(f_high, zl[:, columns]))
+            part_of = folded[two // (n_pz // 4)]
+            both = mm(part_of, zh[:, columns])
+            total = both[:lines] + (both[lines:] + mm(part_of[:lines], zl[:, columns]))
             for t in range(2):
                 j = two * 2 + t
                 tile = total[:, t * LANES : (t + 1) * LANES]
@@ -465,14 +484,22 @@
             low = jnp.where(first, left, pltpu.roll(other, GROUP, 1))
             high = jnp.where(first, pltpu.roll(left, GROUP, 1), other)
             pieces.append(jnp.concatenate((low, high), axis=0))
-        columns = pl.ds(pl.multiple_of(half * NZP, NZP), NZP)
-        return mm_left(jnp.concatenate(pieces, axis=1), zh[:, columns], zl[:, columns], right)
+        given = []
+        for odd_part in range(2):
+            columns = pl.ds(pl.multiple_of(half * NZP + odd_part * (NZP // 2), NZP // 2), NZP // 2)
+            group = pieces[odd_part * n_pz // 2 : (odd_part + 1) * n_pz // 2]
+            given.append(mm_left(jnp.concatenate(group, axis=1), zh[:, columns], zl[:, columns], right))
+        return given
 
     wait_near(back_send, back_recv, 4)
-    phi = side_phi(near)
+    near_phi = side_phi(near)
     wait_far(back_send, back_recv, 4)
-    phi = phi + side_phi(far)
-    phi = jnp.concatenate([phi[:, c * LANES : (c + 1) * LANES] for c in range(NZP // LANES)], axis=0)
+    even, odd_sum = [one_side + other for one_side, other in zip(near_phi, side_phi(far))]
+    front, rear = even + odd_sum, even - odd_sum
+    front = [front[:, c * LANES : (c + 1) * LANES] for c in range(pieces_z // 2)]
+    rear = [rear[:, c * LANES : (c + 1) * LANES] for c in range(pieces_z // 2 - 1, -1, -1)]
+    m_high, m_low = halves(jnp.concatenate(rear, axis=0))
+    phi = jnp.concatenate((*front, mm(m_high, mirror) + mm(m_low, mirror)), axis=0)
     out_send[...] = mm_pick(taking, phi).reshape(n_dev, cap, LANES)
     send_all(out_send, out_recv, 5)
     unpacking = one(place == iota((slots, rows), 1).astype(jnp.float32))
@@ -499,8 +526,8 @@
     slots = charge.shape[0]
     cap = 2 * slots // n_dev
     y_table, x_table = plane_tables(n_px, n_pz)
-    z_table = long_table().reshape(NZP, n_pz, 2, 2 * GROUP).transpose(0, 2, 1, 3)
-    z_table = z_table.reshape(NZP, 2 * NZP) / math.sqrt(2 * NZP)
+    z_table = folded_table().reshape(NZP // 2, n_pz, 2, 2 * GROUP).transpose(0, 2, 1, 3)
+    z_table = z_table.reshape(NZP // 2, 2 * NZP)
     tables = [
         piece
         for table in (z_table, y_table, x_table)
@@ -525,6 +552,7 @@
             *exchange(n_dev, 16),
             *exchange(n_dev, cap),
             pltpu.VMEM((2 * n_px * GROUP, 2 * HALF * KEPT), jnp.float32),
+            pltpu.VMEM((2, 2 * CXP * CYP, NZP // 2), jnp.bfloat16),
             pltpu.SemaphoreType.DMA((7,)),
             pltpu.SemaphoreType.DMA((5,)),
             pltpu.SemaphoreType.DMA((6,)),

time: 50.7 us -> 49.6 us (0.978)
  Pallas kernels: 49 us -> 47.9 us
    pallas_call x1, Pallas kernels: 49 us -> 47.9 us  [local_fused(): pl.pallas_call(functools.partial(fused, n_px, n_pz), out_shape=jax.ShapeD...]
where the time goes in v5:
time: 49.6 us; the launch traced here: 49.5 us
  Pallas kernels  47.9 us (97%)
  local copies, waits for them, and re-layouts  1.57 us (3%)
    pallas_call x1, Pallas kernels, local_fused(): pl.pallas_call(functools.partial(fused, n_px, n_pz), out_shape=jax.ShapeD...  47.9 us
    unnamed x1, local copies, waits for them, and re-layouts  1.57 us

profile of v5, /device:TPU:0, one launch (start us, length us, event | category | flops | bytes accessed | tf_op | source)
XLA Modules:
  0.0 49.5 jit_solution(17145789867712115179)
XLA Ops:
  0.0 47.9 %shard_map.100 = f32[256,128]{1,0:T(8,128)} custom-call(f32[256,128]{1,0:T(8,128)} %charge_ref.1, s32[1,256]{1,0:T(1,128)} %bitcast.2, s32[1,256]{1,0:T(1,128)} %bitcast.3, f32[64,16,256]{2,1,0:T(8,128)} %green_hbm.1, bf16[512,2048]{1,0:T(8,128)(2,1)} %constant.12.clone.zh_hbm, bf16[512,2048]{1,0:T(8,128)(2,1)} %constant.13.clone.zl_hbm, ...), custom_call_target="tpu_custom_call" | custom-call | tf_op jit(solution)/shard_map/pallas_call | solution.py:538
  47.9 1.6 %copy.12 = f32[256,128]{1,0:T(8,128)} copy(f32[256,128]{1,0:T(8,128)} %shard_map.100) | data formatting | bytes 262144

commit v6 on v5

--- a/solution.py
+++ b/solution.py
@@ -272,8 +272,14 @@
         recv[me] = send[me]
 
     def send_all(send, recv, number):
-        send_far(send, recv, number)
-        send_near(send, recv, number)
+        def body(step, carry):
+            block_copy(send, recv, number, far * side + lax.rem(me + step, side), 1).start()
+            block_copy(send, recv, number, near * side + lax.rem(me + step, side), 0).start()
+            return carry
+
+        block_copy(send, recv, number, far * side + lax.rem(me, side), 1).start()
+        lax.fori_loop(1, side, body, 0)
+        recv[me] = send[me]
 
     def all_of(send, recv, number, count, part=0):
         return pltpu.make_async_remote_copy(
@@ -346,17 +352,19 @@
     green_recv[odd] = green_send[mi]
 
     wait_both(ids_send, ids_recv, 0)
-    line = iota((rows, n_dev), 0)
-    spread = mm(one(line // cap == iota((rows, n_dev), 1)), ids_recv[...].reshape(n_dev, LANES).astype(jnp.bfloat16))
-    own_lane = iota((rows, LANES), 1) == lax.rem(iota((rows, LANES), 0), cap)
+    line = iota((rows, 1), 0)
+    cap_bits, line_bits = cap.bit_length() - 1, (CXP * CYP).bit_length() - 1
+    from_box = one((line >> cap_bits) == iota((1, n_dev), 1))
+    spread = mm(from_box, ids_recv[...].reshape(n_dev, LANES).astype(jnp.bfloat16))
+    own_lane = (line & (cap - 1)) == iota((1, LANES), 1)
     ids = jnp.sum(jnp.where(own_lane, spread, 0.0), axis=1, keepdims=True)
     lines = CXP * CYP
 
     def target_of(index):
-        return (lax.rem(index, lines) * (NZP // LANES) + index // lines + 1).astype(jnp.float32)
-
-    taking = one(ids == target_of(iota((rows, blocks), 1)))
-    placing = one(as_row(ids) == target_of(iota((blocks, rows), 0)))
+        return ((index & (lines - 1)) * (NZP // LANES) + (index >> line_bits) + 1).astype(jnp.float32)
+
+    taking = one(ids == target_of(iota((1, blocks), 1)))
+    placing = one(as_row(ids) == target_of(iota((blocks, 1), 0)))
     wait_both(charge_send, charge_recv, 1)
     field = mm_pick(placing, charge_recv[...].reshape(rows, LANES))
     mirror = one(iota((LANES, LANES), 0) + iota((LANES, LANES), 1) == LANES - 1)
@@ -404,15 +412,16 @@
 
         lax.fori_loop(0, n_pz // 2, body, 0)
 
+    forward(near, 0)
     forward(far, 1)
-    forward(near, 0)
     spec_recv[me] = spec_send[me]
 
     green_copy.wait_recv()
     edge_copy(0).wait_recv()
-    source, target = iota((LANES, 512), 0), iota((LANES, 512), 1)
-    wanted = jnp.where(target == 256, HALF, lax.rem(target, 256) // KEPT) + 2 * KEPT
-    picking = one((source == wanted) & (lax.rem(target, KEPT) == 0))
+    target = iota((1, 512), 1)
+    wanted = jnp.where(target == 256, HALF, (target & 255) >> 3) + 2 * KEPT
+    wanted = jnp.where((target & (KEPT - 1)) == 0, wanted, -1)
+    picking = one(iota((LANES, 1), 0) == wanted)
     e_high, e_low = halves(edge_recv[...])
     lone = mm(e_high, picking) + mm(e_low, picking)
     lane = iota((GROUP, LANES), 1)
@@ -426,7 +435,7 @@
             at = (2 * parity + t) * GROUP
             scale[at : at + GROUP, :] = full
             if parity == 0 and t == 0:
-                full = jnp.where(lax.rem(iota((GROUP, 512), 1), KEPT) == 0, lone, full)
+                full = jnp.where((target & (KEPT - 1)) == 0, lone, full)
             at = at + n_px * GROUP
             scale[at : at + GROUP, :] = full
 
@@ -472,10 +481,10 @@
         given = mm(high, p_high, right) + (mm(high, p_low, right) + mm(low, p_high, right))
         back_send[pl.ds(half * side, side)] = given.reshape(side, 16, LANES)
 
+    side_back(near)
+    send_near(back_send, back_recv, 4)
     side_back(far)
     send_far(back_send, back_recv, 4)
-    side_back(near)
-    send_near(back_send, back_recv, 4)
 
     def side_phi(half):
         pieces = []

time: 49.6 us -> 51.1 us (1.030)
  Pallas kernels: 47.9 us -> 49.4 us
    pallas_call x1, Pallas kernels: 47.9 us -> 49.4 us  [local_fused(): pl.pallas_call(functools.partial(fused, n_px, n_pz), out_shape=jax.ShapeD...]
where the time goes in v6:
time: 51.1 us; the launch traced here: 51 us
  Pallas kernels  49.4 us (97%)
  local copies, waits for them, and re-layouts  1.57 us (3%)
    pallas_call x1, Pallas kernels, local_fused(): pl.pallas_call(functools.partial(fused, n_px, n_pz), out_shape=jax.ShapeD...  49.4 us
    unnamed x1, local copies, waits for them, and re-layouts  1.57 us

profile of v6, /device:TPU:0, one launch (start us, length us, event | category | flops | bytes accessed | tf_op | source)
XLA Modules:
  0.0 51.0 jit_solution(12935724076521411867)
XLA Ops:
  0.0 49.4 %shard_map.100 = f32[256,128]{1,0:T(8,128)} custom-call(f32[256,128]{1,0:T(8,128)} %charge_ref.1, s32[1,256]{1,0:T(1,128)} %bitcast.2, s32[1,256]{1,0:T(1,128)} %bitcast.3, f32[64,16,256]{2,1,0:T(8,128)} %green_hbm.1, bf16[512,2048]{1,0:T(8,128)(2,1)} %constant.12.clone.zh_hbm, bf16[512,2048]{1,0:T(8,128)(2,1)} %constant.13.clone.zl_hbm, ...), custom_call_target="tpu_custom_call" | custom-call | tf_op jit(solution)/shard_map/pallas_call | solution.py:547
  49.4 1.6 %copy.12 = f32[256,128]{1,0:T(8,128)} copy(f32[256,128]{1,0:T(8,128)} %shard_map.100) | data formatting | bytes 262144

commit v7 on v6

--- a/solution.py
+++ b/solution.py
@@ -211,7 +211,7 @@
 def fused(
     n_px, n_pz, charge_ref, dest_ref, ids_ref, green_hbm, zh_hbm, zl_hbm, yh_hbm, yl_hbm, xh_hbm,
     xl_hbm, out_ref, green, zh, zl, yh, yl, xh, xl, ids_send, ids_recv, charge_send, charge_recv,
-    green_send, green_recv, edge_recv, spec_send, spec_recv, back_send, back_recv, out_send, out_recv, scale, folded,
+    green_send, green_recv, edge_recv, spec_send, spec_recv, back_send, back_recv, out_send, out_recv, scale, folded, taking,
     load_sems, green_sems, send_sems, recv_sems
 ):
     n_dev = n_px * n_pz
@@ -272,14 +272,8 @@
         recv[me] = send[me]
 
     def send_all(send, recv, number):
-        def body(step, carry):
-            block_copy(send, recv, number, far * side + lax.rem(me + step, side), 1).start()
-            block_copy(send, recv, number, near * side + lax.rem(me + step, side), 0).start()
-            return carry
-
-        block_copy(send, recv, number, far * side + lax.rem(me, side), 1).start()
-        lax.fori_loop(1, side, body, 0)
-        recv[me] = send[me]
+        send_far(send, recv, number)
+        send_near(send, recv, number)
 
     def all_of(send, recv, number, count, part=0):
         return pltpu.make_async_remote_copy(
@@ -311,11 +305,19 @@
     owned = jnp.where(dest_row == iota((n_dev, slots), 0).astype(jnp.float32), ids, 0.0)
     ranked = one(rank == iota((slots, LANES), 1).astype(jnp.float32))
     ids_send[...] = mm(owned.astype(jnp.bfloat16), ranked).reshape(n_dev, 1, LANES)
-    packing = one(as_row(place) == iota((rows, slots), 0).astype(jnp.float32))
-    charge_send[...] = mm_pick(packing, charge_ref[...]).reshape(n_dev, cap, LANES)
+    place_row = as_row(place)
+
+    def pack(half):
+        places = (iota((side * cap, 1), 0) + half * (side * cap)).astype(jnp.float32)
+        packed = mm_pick(one(place_row == places), charge_ref[...])
+        charge_send[pl.ds(half * side, side)] = packed.reshape(side, cap, LANES)
+
+    pack(far)
     pl.semaphore_wait(barrier, n_dev - 1)
     send_all(ids_send, ids_recv, 0)
-    send_all(charge_send, charge_recv, 1)
+    send_far(charge_send, charge_recv, 1)
+    pack(near)
+    send_near(charge_send, charge_recv, 1)
 
     loads[0].wait()
     wide = [jnp.transpose(green[0:HALF, t * KEPT : (t + 1) * KEPT, :].reshape(HALF * KEPT, 256)) for t in range(2)]
@@ -363,7 +365,7 @@
     def target_of(index):
         return ((index & (lines - 1)) * (NZP // LANES) + (index >> line_bits) + 1).astype(jnp.float32)
 
-    taking = one(ids == target_of(iota((1, blocks), 1)))
+    taking[...] = one(ids == target_of(iota((1, blocks), 1)))
     placing = one(as_row(ids) == target_of(iota((blocks, 1), 0)))
     wait_both(charge_send, charge_recv, 1)
     field = mm_pick(placing, charge_recv[...].reshape(rows, LANES))
@@ -412,8 +414,8 @@
 
         lax.fori_loop(0, n_pz // 2, body, 0)
 
+    forward(far, 1)
     forward(near, 0)
-    forward(far, 1)
     spec_recv[me] = spec_send[me]
 
     green_copy.wait_recv()
@@ -475,16 +477,24 @@
     p_high, p_low = halves(planes)
     right = ((1,), (1,))
 
-    def side_back(half):
-        table_rows = pl.ds(pl.multiple_of(half * (side * 16), side * 16), side * 16)
+    def row_back(i):
+        table_rows = pl.ds(pl.multiple_of(i * (n_pz * 16), n_pz * 16), n_pz * 16)
         high, low = yh[table_rows, :], yl[table_rows, :]
         given = mm(high, p_high, right) + (mm(high, p_low, right) + mm(low, p_high, right))
-        back_send[pl.ds(half * side, side)] = given.reshape(side, 16, LANES)
-
-    side_back(near)
+        back_send[pl.ds(i * n_pz, n_pz)] = given.reshape(n_pz, 16, LANES)
+
+    for turn in range(2):
+        line_i = far * 2 + lax.rem(mi + turn, 2)
+        row_back(line_i)
+
+        def send_row(step, carry, line_i=line_i):
+            block_copy(back_send, back_recv, 4, line_i * n_pz + lax.rem(mj + step, n_pz), 1).start()
+            return carry
+
+        lax.fori_loop(0, n_pz, send_row, 0)
+    for turn in range(2):
+        row_back(near * 2 + turn)
     send_near(back_send, back_recv, 4)
-    side_back(far)
-    send_far(back_send, back_recv, 4)
 
     def side_phi(half):
         pieces = []
@@ -509,8 +519,17 @@
     rear = [rear[:, c * LANES : (c + 1) * LANES] for c in range(pieces_z // 2 - 1, -1, -1)]
     m_high, m_low = halves(jnp.concatenate(rear, axis=0))
     phi = jnp.concatenate((*front, mm(m_high, mirror) + mm(m_low, mirror)), axis=0)
-    out_send[...] = mm_pick(taking, phi).reshape(n_dev, cap, LANES)
-    send_all(out_send, out_recv, 5)
+    phi_high, phi_low = halves(phi)
+
+    def take(half):
+        one_hot = taking[pl.ds(pl.multiple_of(half * (side * cap), side * cap), side * cap), :]
+        taken = mm(one_hot, phi_high) + mm(one_hot, phi_low)
+        out_send[pl.ds(half * side, side)] = taken.reshape(side, cap, LANES)
+
+    take(far)
+    send_far(out_send, out_recv, 5)
+    take(near)
+    send_near(out_send, out_recv, 5)
     unpacking = one(place == iota((slots, rows), 1).astype(jnp.float32))
     wait_both(out_send, out_recv, 5)
     out_ref[...] = mm_pick(unpacking, out_recv[...].reshape(rows, LANES))
@@ -562,6 +581,7 @@
             *exchange(n_dev, cap),
             pltpu.VMEM((2 * n_px * GROUP, 2 * HALF * KEPT), jnp.float32),
             pltpu.VMEM((2, 2 * CXP * CYP, NZP // 2), jnp.bfloat16),
+            pltpu.VMEM((n_dev * cap, CXP * CYP * NZP // LANES), jnp.bfloat16),
             pltpu.SemaphoreType.DMA((7,)),
             pltpu.SemaphoreType.DMA((5,)),
             pltpu.SemaphoreType.DMA((6,)),

time: 51.1 us -> 47.9 us (0.937)
  Pallas kernels: 49.4 us -> 46.2 us
    pallas_call x1, Pallas kernels: 49.4 us -> 46.2 us  [local_fused(): pl.pallas_call(functools.partial(fused, n_px, n_pz), out_shape=jax.ShapeD...]
where the time goes in v7:
time: 47.9 us; the launch traced here: 47.8 us
  Pallas kernels  46.2 us (96%)
  local copies, waits for them, and re-layouts  1.57 us (3%)
    pallas_call x1, Pallas kernels, local_fused(): pl.pallas_call(functools.partial(fused, n_px, n_pz), out_shape=jax.ShapeD...  46.2 us
    unnamed x1, local copies, waits for them, and re-layouts  1.57 us

profile of v7, /device:TPU:0, one launch (start us, length us, event | category | flops | bytes accessed | tf_op | source)
XLA Modules:
  0.0 47.8 jit_solution(8615461803152801464)
XLA Ops:
  0.0 46.2 %shard_map.100 = f32[256,128]{1,0:T(8,128)} custom-call(f32[256,128]{1,0:T(8,128)} %charge_ref.1, s32[1,256]{1,0:T(1,128)} %bitcast.2, s32[1,256]{1,0:T(1,128)} %bitcast.3, f32[64,16,256]{2,1,0:T(8,128)} %green_hbm.1, bf16[512,2048]{1,0:T(8,128)(2,1)} %constant.12.clone.zh_hbm, bf16[512,2048]{1,0:T(8,128)(2,1)} %constant.13.clone.zl_hbm, ...), custom_call_target="tpu_custom_call" | custom-call | tf_op jit(solution)/shard_map/pallas_call | solution.py:566
  46.2 1.6 %copy.12 = f32[256,128]{1,0:T(8,128)} copy(f32[256,128]{1,0:T(8,128)} %shard_map.100) | data formatting | bytes 262144

commit v8 on v7

--- a/solution.py
+++ b/solution.py
@@ -257,18 +257,12 @@
         )
 
     def send_far(send, recv, number):
-        def body(step, carry):
+        for step in range(side):
             block_copy(send, recv, number, far * side + lax.rem(me + step, side), 1).start()
-            return carry
-
-        lax.fori_loop(0, side, body, 0)
 
     def send_near(send, recv, number):
-        def body(step, carry):
+        for step in range(1, side):
             block_copy(send, recv, number, near * side + lax.rem(me + step, side), 0).start()
-            return carry
-
-        lax.fori_loop(1, side, body, 0)
         recv[me] = send[me]
 
     def send_all(send, recv, number):
@@ -486,12 +480,8 @@
     for turn in range(2):
         line_i = far * 2 + lax.rem(mi + turn, 2)
         row_back(line_i)
-
-        def send_row(step, carry, line_i=line_i):
+        for step in range(n_pz):
             block_copy(back_send, back_recv, 4, line_i * n_pz + lax.rem(mj + step, n_pz), 1).start()
-            return carry
-
-        lax.fori_loop(0, n_pz, send_row, 0)
     for turn in range(2):
         row_back(near * 2 + turn)
     send_near(back_send, back_recv, 4)

time: 47.9 us -> 47.4 us (0.990)
  Pallas kernels: 46.2 us -> 45.7 us
    pallas_call x1, Pallas kernels: 46.2 us -> 45.7 us  [local_fused(): pl.pallas_call(functools.partial(fused, n_px, n_pz), out_shape=jax.ShapeD...]
where the time goes in v8:
time: 47.4 us; the launch traced here: 47.3 us
  Pallas kernels  45.7 us (96%)
  local copies, waits for them, and re-layouts  1.57 us (3%)
    pallas_call x1, Pallas kernels, local_fused(): pl.pallas_call(functools.partial(fused, n_px, n_pz), out_shape=jax.ShapeD...  45.7 us
    unnamed x1, local copies, waits for them, and re-layouts  1.57 us

profile of v8, /device:TPU:0, one launch (start us, length us, event | category | flops | bytes accessed | tf_op | source)
XLA Modules:
  0.0 47.3 jit_solution(15927783434066455154)
XLA Ops:
  0.0 45.7 %shard_map.100 = f32[256,128]{1,0:T(8,128)} custom-call(f32[256,128]{1,0:T(8,128)} %charge_ref.1, s32[1,256]{1,0:T(1,128)} %bitcast.2, s32[1,256]{1,0:T(1,128)} %bitcast.3, f32[64,16,256]{2,1,0:T(8,128)} %green_hbm.1, bf16[512,2048]{1,0:T(8,128)(2,1)} %constant.12.clone.zh_hbm, bf16[512,2048]{1,0:T(8,128)(2,1)} %constant.13.clone.zl_hbm, ...), custom_call_target="tpu_custom_call" | custom-call | tf_op jit(solution)/shard_map/pallas_call | solution.py:556
  45.7 1.6 %copy.12 = f32[256,128]{1,0:T(8,128)} copy(f32[256,128]{1,0:T(8,128)} %shard_map.100) | data formatting | bytes 262144
